TPU v7x, 32 devices: a whole 2x2x4 slice. The times are simulated.
32 devices in a mesh: dp: 2 (over y), expert: 16 (over z, x, core).
Axes of the slice: x: 2, y: 2, z: 4, core: 2. Of those that a mesh axis runs over, the one named last changes fastest.
Arguments:
- tokens: bfloat16 [2048, 1024], P('expert'), may hold values from -6 to 6
- routes: int32 [2048, 6], P('expert'), may hold values from 0 to 15, all different within a row; in each aligned block of 128 rows (0 to 127, 128 to 255, ...) at most 64 rows name the same one
- route_gates: bfloat16 [2048, 6], P('expert'), may hold values from 0.049804688 to 0.5
- domains: int32 [2048], P('expert'), may hold values from 0 to 63
- domain_weight: float32 [64], replicated, may hold values from 0.25 to 4
- targets: bfloat16 [2048, 1024], P('expert'), may hold values from -6 to 6
- w_gate: bfloat16 [16, 1024, 1024], P('expert', None, 'dp'), may hold values from -0.1875 to 0.1875
- w_up: bfloat16 [16, 1024, 1024], P('expert', None, 'dp'), may hold values from -0.1875 to 0.1875
- w_down: bfloat16 [16, 1024, 1024], P('expert', 'dp'), may hold values from -0.1875 to 0.1875
Outputs:
- grad_tokens: bfloat16 [2048, 1024], P('expert')
- grad_gate: float32 [16, 1024, 1024], P('expert', None, 'dp')
- grad_up: float32 [16, 1024, 1024], P('expert', None, 'dp')
- grad_down: float32 [16, 1024, 1024], P('expert', 'dp')
Inputs may be any that keep to these rules, and one draw needn't show every extreme that they name: `routes`: each row names 6 different experts. Among the rows of one block of 128 tokens no expert is named more than 64 times, and in every draw some block names some expert exactly 64 times.
All inputs are finite; a program needn't handle non-finite values.
Results may differ from a plain program's by a relative error of at most 0.015.
Values may be sent and summed in bfloat16 or wider, within the bound.
A program may use at most 64 MiB of HBM per device.

v0:
```python
import jax
import jax.numpy as jnp
from jax import lax
from jax.sharding import PartitionSpec as P


def positions(flat_routes, experts):
    onehot = (flat_routes[:, None] == jnp.arange(experts, dtype=jnp.int32)[None, :]).astype(
        jnp.int32
    )
    return jnp.sum((jnp.cumsum(onehot, 0) - onehot) * onehot, 1)


def tables(routes, route_gates, experts, capacity):
    flat_routes = routes.reshape(-1)
    places = positions(flat_routes, experts)
    slot_ids = (flat_routes * capacity + places).reshape(routes.shape)
    matches = slot_ids[None, :, :] == jnp.arange(experts * capacity, dtype=jnp.int32)[:, None, None]
    select = jnp.any(matches, 2).astype(jnp.bfloat16)
    gated_select = jnp.sum(
        jnp.where(matches, route_gates.astype(jnp.float32)[None, :, :], 0.0), 2
    ).astype(jnp.bfloat16)
    return (select, gated_select)


def expert_forward(slot_rows, w_gate, w_up, w_down):
    gate_pre = jnp.dot(slot_rows, w_gate[0], preferred_element_type=jnp.float32)
    up_pre = jnp.dot(slot_rows, w_up[0], preferred_element_type=jnp.float32)
    hidden = (jax.nn.silu(gate_pre) * up_pre).astype(jnp.bfloat16)
    slot_part = jnp.dot(hidden, w_down[0], preferred_element_type=jnp.float32).astype(jnp.bfloat16)
    return (gate_pre, up_pre, hidden, slot_part)


def expert_backward(slot_rows, slot_grads, gate_pre, up_pre, hidden, w_gate, w_up, w_down):
    contract_last = (((1,), (1,)), ((), ()))
    contract_first = (((0,), (0,)), ((), ()))
    hidden_grad = lax.dot_general(
        slot_grads, w_down[0], contract_last, preferred_element_type=jnp.float32
    )
    sigma = jax.nn.sigmoid(gate_pre)
    gate_grad = (hidden_grad * up_pre * sigma * (1.0 + gate_pre * (1.0 - sigma))).astype(
        jnp.bfloat16
    )
    up_grad = (hidden_grad * gate_pre * sigma).astype(jnp.bfloat16)
    grad_down = lax.dot_general(
        hidden, slot_grads, contract_first, preferred_element_type=jnp.float32
    )
    grad_gate = lax.dot_general(
        slot_rows, gate_grad, contract_first, preferred_element_type=jnp.float32
    )
    grad_up = lax.dot_general(
        slot_rows, up_grad, contract_first, preferred_element_type=jnp.float32
    )
    row_part = lax.dot_general(
        gate_grad, w_gate[0], contract_last, preferred_element_type=jnp.float32
    )
    row_part = row_part + lax.dot_general(
        up_grad, w_up[0], contract_last, preferred_element_type=jnp.float32
    )
    return (grad_gate[None], grad_up[None], grad_down[None], row_part.astype(jnp.bfloat16))


def loss_gradient(layer_out, domains, domain_weight, targets):
    picks = domains[:, None] == jnp.arange(domain_weight.shape[0], dtype=jnp.int32)[None, :]
    scales = jnp.sum(jnp.where(picks, domain_weight[None, :], 0.0), 1)
    return (scales[:, None] * (layer_out - targets.astype(jnp.float32))).astype(jnp.bfloat16)


def shards(tokens, routes, route_gates, domains, domain_weight, targets, w_gate, w_up, w_down):
    per_device = tokens.shape[0]
    top_count = routes.shape[1]
    experts = lax.axis_size("expert") * w_gate.shape[0]
    capacity = max(2, 4 * per_device * top_count // (3 * experts))
    select, gated_select = tables(routes, route_gates, experts, capacity)
    send_rows = jnp.dot(select, tokens, preferred_element_type=jnp.float32).astype(jnp.bfloat16)
    slot_rows = lax.all_to_all(send_rows, "expert", split_axis=0, concat_axis=0, tiled=True)
    gate_pre, up_pre, hidden, slot_part = expert_forward(slot_rows, w_gate, w_up, w_down)
    returned = lax.all_to_all(slot_part, "expert", split_axis=0, concat_axis=0, tiled=True)
    column_out = jnp.dot(gated_select.T, returned, preferred_element_type=jnp.float32)
    layer_out = lax.psum(column_out, "dp")
    loss_grad = loss_gradient(layer_out, domains, domain_weight, targets)
    grad_send = jnp.dot(gated_select, loss_grad, preferred_element_type=jnp.float32).astype(
        jnp.bfloat16
    )
    slot_grads = lax.all_to_all(grad_send, "expert", split_axis=0, concat_axis=0, tiled=True)
    grad_gate, grad_up, grad_down, row_part = expert_backward(
        slot_rows, slot_grads, gate_pre, up_pre, hidden, w_gate, w_up, w_down
    )
    grad_returned = lax.all_to_all(row_part, "expert", split_axis=0, concat_axis=0, tiled=True)
    column_input = jnp.dot(select.T, grad_returned, preferred_element_type=jnp.float32)
    grad_tokens = lax.psum(column_input, "dp")
    return (grad_tokens.astype(jnp.bfloat16), grad_gate, grad_up, grad_down)


def solution(mesh):
    return jax.shard_map(
        shards,
        mesh=mesh,
        in_specs=(
            P("expert", None),
            P("expert", None),
            P("expert", None),
            P("expert"),
            P(),
            P("expert", None),
            P("expert", None, "dp"),
            P("expert", None, "dp"),
            P("expert", "dp", None),
        ),
        out_specs=(
            P("expert", None),
            P("expert", None, "dp"),
            P("expert", None, "dp"),
            P("expert", "dp", None),
        ),
        check_vma=False,
    )
```

profile of v0, /device:TPU:0, one launch (start us, length us, event | category | flops | bytes accessed | tf_op | source)
XLA Modules:
  0.0 293.6 jit_solution(5748764652035667232)
XLA Ops:
  7.2 0.9 copy.27
  8.4 1.7 reduce-window.6
  10.7 0.7 multiply_add_fusion
  11.9 1.6 convolution_convert_fusion.2
  13.5 54.6 %all_to_all.48 = bf16[16,64,1024]{2,1,0:T(8,128)(2,1)S(1)} all-to-all(bf16[16,64,1024]{2,1,0:T(8,128)(2,1)S(1)} %bitcast.77), channel_id=1, replica_groups=mesh['dp'=2,'expert'=16] {'expert'}, dimensions={0} | all-to-all | bytes 4194304 | tf_op jit(solution)/shard_map/all_to_all | solution.py:76
  68.2 1.3 fusion.9
  70.1 2.7 multiply_convert_fusion.2
  72.9 2.6 convolution_convert_fusion
  75.5 5.2 %all-to-all-start.1 = ((bf16[16,64,1024]{2,1,0:T(8,128)(2,1)}), bf16[16,64,1024]{2,1,0:T(8,128)(2,1)S(1)}, u32[]{:S(2)}, u32[]{:S(2)}) async-start(bf16[16,64,1024]{2,1,0:T(8,128)(2,1)} %bitcast.83), calls=%async_computation.1 | async-start | bytes 4194304 | tf_op jit(solution)/shard_map/all_to_all | solution.py:78
  81.2 40.6 %all-to-all-done.1 = bf16[16,64,1024]{2,1,0:T(8,128)(2,1)S(1)} async-done(((bf16[16,64,1024]{2,1,0:T(8,128)(2,1)}), bf16[16,64,1024]{2,1,0:T(8,128)(2,1)S(1)}, u32[]{:S(2)}, u32[]{:S(2)}) %all-to-all-start.1) | async-done | bytes 2097184 | tf_op jit(solution)/shard_map/all_to_all | solution.py:78
  121.8 1.3 fusion.20
  123.2 35.2 %all-reduce.3.cloned.1.call-done = f32[128,1024]{1,0:T(8,128)} async-done(((f32[128,1024]{1,0:T(8,128)}), f32[128,1024]{1,0:T(8,128)}) %all-reduce.3.cloned.1.call-update) | async-done | bytes 524304 | tf_op jit(solution)/shard_map/psum | solution.py:80
  158.4 1.9 convolution_convert_fusion.1
  160.3 53.0 %all_to_all.49 = bf16[16,64,1024]{2,1,0:T(8,128)(2,1)S(1)} all-to-all(bf16[16,64,1024]{2,1,0:T(8,128)(2,1)S(1)} %bitcast.76), channel_id=1, replica_groups=mesh['dp'=2,'expert'=16] {'expert'}, dimensions={0} | all-to-all | bytes 4194304 | tf_op jit(solution)/shard_map/all_to_all | solution.py:85
  213.4 1.9 multiply_convert_fusion
  215.4 1.3 fusion.7
  217.3 2.6 add_convert_fusion
  219.9 5.1 %all-to-all-start.3 = ((bf16[16,64,1024]{2,1,0:T(8,128)(2,1)}), bf16[16,64,1024]{2,1,0:T(8,128)(2,1)S(1)}, u32[]{:S(2)}, u32[]{:S(2)}) async-start(bf16[16,64,1024]{2,1,0:T(8,128)(2,1)} %bitcast.78), calls=%async_computation.3 | async-start | bytes 4194304 | tf_op jit(solution)/shard_map/all_to_all | solution.py:89
  225.0 4.6 %convolution_bitcast_fusion = f32[1,512,1024]{2,1,0:T(8,128)} fusion(bf16[1024,512]{1,0:T(8,128)(2,1)} %copy-done.4, bf16[1024,1024]{1,0:T(8,128)(2,1)} %bitcast.74), kind=kOutput, calls=%fused_computation.11 | convolution fusion | flops 1073741824 | bytes 5242880 | tf_op jit(solution)/shard_map/dot_general | solution.py:45
  229.7 2.6 convolution_bitcast_fusion.1
  232.3 2.6 convolution_bitcast_fusion.2
  234.9 31.2 %all-to-all-done.3 = bf16[16,64,1024]{2,1,0:T(8,128)(2,1)S(1)} async-done(((bf16[16,64,1024]{2,1,0:T(8,128)(2,1)}), bf16[16,64,1024]{2,1,0:T(8,128)(2,1)S(1)}, u32[]{:S(2)}, u32[]{:S(2)}) %all-to-all-start.3) | async-done | bytes 2097184 | tf_op jit(solution)/shard_map/all_to_all | solution.py:89
  266.1 1.3 fusion.19
  267.4 19.3 %all-reduce.4 = bf16[128,1024]{1,0:T(8,128)(2,1)} all-reduce(f32[128,1024]{1,0:T(8,128)} %fusion.19), channel_id=1, replica_groups=mesh['dp'=2,'expert'=16] {'dp'}, use_global_device_ids=true, to_apply=%region_7.8 | all-reduce | flops 131072 | bytes 786432 | tf_op jit(solution)/shard_map/psum | solution.py:91
  (52 shorter events, 3.3 us)
Async XLA Ops:
  7.2 65.7 %copy-start = (bf16[1,512,1024]{2,1,0:T(8,128)(2,1)S(1)}, bf16[1,512,1024]{2,1,0:T(8,128)(2,1)}, u32[]{:S(2)}) copy-start(bf16[1,512,1024]{2,1,0:T(8,128)(2,1)} %param.17) | copy-start | bytes 3145732
  13.5 54.6 %copy-start.10 = (bf16[1,1024,512]{2,1,0:T(8,128)(2,1)S(1)}, bf16[1,1024,512]{2,1,0:T(8,128)(2,1)}, u32[]{:S(2)}) copy-start(bf16[1,1024,512]{2,1,0:T(8,128)(2,1)} %param.15) | copy-start | bytes 3145732
  68.1 1.3 copy-start.2
  68.1 2.0 copy-start.5
  70.1 2.8 copy-start.16
  72.9 2.6 copy-start.4
  75.5 5.3 %copy-start.9 = (bf16[128,6]{0,1:T(8,128)(2,1)S(1)}, bf16[128,6]{0,1:T(8,128)(2,1)}, u32[]{:S(2)}) copy-start(bf16[128,6]{0,1:T(8,128)(2,1)} %param.11) | copy-start | bytes 4612
  75.5 46.4 %all-to-all-start.1 = ((bf16[16,64,1024]{2,1,0:T(8,128)(2,1)}), bf16[16,64,1024]{2,1,0:T(8,128)(2,1)S(1)}, u32[]{:S(2)}, u32[]{:S(2)}) async-start(bf16[16,64,1024]{2,1,0:T(8,128)(2,1)} %bitcast.83), calls=%async_computation.1 | async-start | bytes 4194304 | tf_op jit(solution)/shard_map/all_to_all | solution.py:78
  80.7 42.4 %copy-start.12 = (f32[64]{0:T(128)S(1)}, f32[64]{0:T(128)}, u32[]{:S(2)}) copy-start(f32[64]{0:T(128)} %param.13) | copy-start | bytes 772
  80.7 42.4 %copy-start.13 = (s32[128]{0:T(128)S(1)}, s32[128]{0:T(128)}, u32[]{:S(2)}) copy-start(s32[128]{0:T(128)} %param.12) | copy-start | bytes 1540
  80.8 77.7 %all-reduce.3.cloned.1.call-start = ((), (), s32[]{:S(2)}) async-start(), calls=%async_computation.4 | async-start | bytes 1048576 | tf_op jit(solution)/shard_map/psum | solution.py:80
  160.3 53.0 %copy-start.17 = (f32[1024,512]{1,0:T(8,128)S(1)}, f32[1024,512]{1,0:T(8,128)}, u32[]{:S(2)}) copy-start(f32[1024,512]{1,0:T(8,128)} %copy-done.16) | copy-start | bytes 6291460
  160.3 53.0 %copy-start.18 = (f32[1024,512]{1,0:T(8,128)S(1)}, f32[1024,512]{1,0:T(8,128)}, u32[]{:S(2)}) copy-start(f32[1024,512]{1,0:T(8,128)} %get-tuple-element.7) | copy-start | bytes 6291460
  213.3 2.0 copy-start.1
  213.3 2.0 copy-start.11
  215.3 1.3 copy-start.14
  215.3 1.3 copy-start.7
  215.3 2.0 copy-start.6
  219.9 46.2 %all-to-all-start.3 = ((bf16[16,64,1024]{2,1,0:T(8,128)(2,1)}), bf16[16,64,1024]{2,1,0:T(8,128)(2,1)S(1)}, u32[]{:S(2)}, u32[]{:S(2)}) async-start(bf16[16,64,1024]{2,1,0:T(8,128)(2,1)} %bitcast.78), calls=%async_computation.3 | async-start | bytes 4194304 | tf_op jit(solution)/shard_map/all_to_all | solution.py:89
  225.0 4.7 %copy-start.3 = (bf16[16,64,1024]{2,1,0:T(8,128)(2,1)S(1)}, bf16[16,64,1024]{2,1,0:T(8,128)(2,1)}, u32[]{:S(2)}) copy-start(bf16[16,64,1024]{2,1,0:T(8,128)(2,1)} %copy-done.2) | copy-start | bytes 6291460
  225.0 4.7 %copy-start.8 = (bf16[1024,512]{1,0:T(8,128)(2,1)S(1)}, bf16[1024,512]{1,0:T(8,128)(2,1)}, u32[]{:S(2)}) copy-start(bf16[1024,512]{1,0:T(8,128)(2,1)} %copy-done.7) | copy-start | bytes 3145732
  229.7 2.6 copy-start.15
Sparse Core Ops, SparseCore 0:
  123.3 35.1 all-reduce.2
where the time goes:
time: 298 us; the launch traced here: 294 us
  blocking collectives  127 us (43%)
  waiting for transfers between devices  107 us (36%)
  matrix products  28.3 us (9%)
  between operations  14.3 us (5%)
  starting transfers between devices  10.4 us (3%)
  other arithmetic  3.53 us (1%)
  local copies, waits for them, and re-layouts  3.06 us (1%)
    all_to_all x1, blocking collectives, shards(): lax.all_to_all(send_rows, 'expert', split_axis=0, concat_axis=0, tiled=True)  54.6 us
    all_to_all x1, blocking collectives, shards(): lax.all_to_all(grad_send, 'expert', split_axis=0, concat_axis=0, tiled=True)  53 us
    all_to_all x1, waiting for transfers between devices, shards(): lax.all_to_all(slot_part, 'expert', split_axis=0, concat_axis=0, tiled=True)  40.6 us
    psum x1, waiting for transfers between devices, shards(): layer_out = lax.psum(column_out, 'dp')  35.2 us
    all_to_all x1, waiting for transfers between devices, shards(): lax.all_to_all(row_part, 'expert', split_axis=0, concat_axis=0, tiled=True)  31.2 us
    psum x1, blocking collectives, shards(): grad_tokens = lax.psum(column_input, 'dp')  19.3 us
  transfers between devices with their start and end apart: 3, of which 3 were waited for; matrix products, arithmetic and copies ran while one was open for 4% of the time, Pallas kernels for 0%

commit v1 on v0

v1 whole, which is shorter than its diff:
```python
import functools

import jax
import jax.numpy as jnp
from jax import lax
from jax.experimental import pallas as pl
from jax.experimental.pallas import tpu as pltpu
from jax.sharding import PartitionSpec as P

MESH = pl.DeviceIdType.MESH
CORES = 2
COLUMNS = 2
HALVES = 2
UP, DOWN, ACROSS, SIBLING = range(4)


class Place:
    def __init__(self, n):
        self.n = n
        self.height = n // (CORES * COLUMNS)
        self.me = lax.axis_index("expert")
        self.core = lax.rem(self.me, CORES)
        self.x = lax.rem(self.me // CORES, COLUMNS)
        self.z = self.me // (CORES * COLUMNS)
        self.up = self.me + CORES * COLUMNS
        self.down = self.me - CORES * COLUMNS
        self.has_up = self.z + 1 < self.height
        self.has_down = self.z > 0
        self.across = self.at(self.z, 1 - self.x, self.core)
        self.sibling = self.at(self.z, self.x, 1 - self.core)

    def at(self, z, x, core):
        return (z * COLUMNS + x) * CORES + core

    def by_distance(self, d):
        if d == 0:
            return [(self.z, None)]
        return [(self.z - d, self.z - d >= 0), (self.z + d, self.z + d < self.height)]


def when(condition, body):
    if condition is None:
        body()
    else:
        pl.when(condition)(body)


def greet(place, dp_too):
    barrier = pltpu.get_barrier_semaphore()

    def signal(target):
        pl.semaphore_signal(barrier, inc=1, device_id=target, device_id_type=MESH)

    pl.when(place.has_up)(lambda: signal({"expert": place.up}))
    pl.when(place.has_down)(lambda: signal({"expert": place.down}))
    signal({"expert": place.across})
    signal({"expert": place.sibling})
    count = 2 + place.has_up.astype(jnp.int32) + place.has_down.astype(jnp.int32)
    if dp_too:
        dps = lax.axis_size("dp")
        mine = lax.axis_index("dp")
        for step in range(1, dps):
            signal({"dp": lax.rem(mine + step, dps)})
        count = count + (dps - 1)
    pl.semaphore_wait(barrier, count)


def gather(place, pieces, send, recv):
    links = {
        UP: (place.up, place.has_up),
        DOWN: (place.down, place.has_down),
        ACROSS: (place.across, None),
        SIBLING: (place.sibling, None),
    }

    def copy(piece, block, link):
        view = pieces[piece](block)
        return pltpu.make_async_remote_copy(
            src_ref=view,
            dst_ref=view,
            send_sem=send.at[piece, link, block],
            recv_sem=recv.at[piece, block],
            device_id={"expert": links[link][0]},
            device_id_type=MESH,
        )

    def start(piece, block, which):
        for link in which:
            when(links[link][1], lambda link=link: copy(piece, block, link).start())

    def arrive(piece, block):
        copy(piece, block, SIBLING).wait_recv()

    def mine(z):
        return place.at(z, place.x, place.core)

    def other(z):
        return place.at(z, 1 - place.x, place.core)

    def from_across(d):
        for piece in range(len(pieces)):
            for z, there in place.by_distance(d):

                def body(z=z, piece=piece):
                    arrive(piece, other(z))
                    start(piece, other(z), (SIBLING,))

                when(there, body)

    for piece in range(len(pieces)):
        start(piece, place.me, (UP, DOWN, ACROSS, SIBLING))
    for d in range(1, place.height):
        for piece in range(len(pieces)):
            for (z, there), onward in zip(place.by_distance(d), (UP, DOWN)):

                def body(z=z, piece=piece, onward=onward):
                    arrive(piece, mine(z))
                    start(piece, mine(z), (onward, ACROSS, SIBLING))

                when(there, body)
        from_across(d - 1)
    from_across(place.height - 1)

    def finish():
        for z in range(place.height):
            for piece in range(len(pieces)):
                for x in range(COLUMNS):
                    arrive(piece, place.at(z, x, 1 - place.core))
                copy(piece, mine(z), ACROSS).wait_send()
                copy(piece, mine(z), SIBLING).wait_send()
                copy(piece, other(z), SIBLING).wait_send()
                pl.when(jnp.logical_and(place.has_up, z <= place.z))(
                    lambda: copy(piece, mine(z), UP).wait_send()
                )
                pl.when(jnp.logical_and(place.has_down, z >= place.z))(
                    lambda: copy(piece, mine(z), DOWN).wait_send()
                )

    finish()


def scatter(place, part_ref, bufs, sems, leave):
    core_in, across_out, across_in, line_out, line_in, dp_in = bufs
    core_send, core_recv, across_send, across_recv, line_send, line_recv, dp_send, dp_recv = sems
    height = place.height
    rows = part_ref.shape[1] // HALVES
    dps = lax.axis_size("dp")
    dp = lax.axis_index("dp")
    spans = [pl.ds(h * rows, rows) for h in range(HALVES)]
    f32 = jnp.float32

    def core_copy(z, x, h):
        spot = z * COLUMNS + x
        return pltpu.make_async_remote_copy(
            src_ref=part_ref.at[place.at(z, x, 1 - place.core), spans[h]],
            dst_ref=core_in.at[spot, spans[h]],
            send_sem=core_send.at[spot, h],
            recv_sem=core_recv.at[spot, h],
            device_id={"expert": place.sibling},
            device_id_type=MESH,
        )

    def across_copy(z, h):
        return pltpu.make_async_remote_copy(
            src_ref=across_out.at[z, spans[h]],
            dst_ref=across_in.at[z, spans[h]],
            send_sem=across_send.at[z, h],
            recv_sem=across_recv.at[z, h],
            device_id={"expert": place.across},
            device_id_type=MESH,
        )

    def line_copy(z, slot, h, target):
        return pltpu.make_async_remote_copy(
            src_ref=line_out.at[z, spans[h]],
            dst_ref=line_in.at[slot, spans[h]],
            send_sem=line_send.at[z, h],
            recv_sem=line_recv.at[slot, h],
            device_id={"expert": target},
            device_id_type=MESH,
        )

    def line_arrive(slot, h):
        line_copy(0, slot, h, place.up).wait_recv()

    def dp_copy(step, h):
        return pltpu.make_async_remote_copy(
            src_ref=dp_in.at[dp, spans[h]],
            dst_ref=dp_in.at[dp, spans[h]],
            send_sem=dp_send.at[step, h],
            recv_sem=dp_recv.at[dp, h],
            device_id={"dp": lax.rem(dp + step, dps)},
            device_id_type=MESH,
        )

    def dp_arrive(index, h):
        pltpu.make_async_remote_copy(
            src_ref=dp_in.at[dp, spans[h]],
            dst_ref=dp_in.at[index, spans[h]],
            send_sem=dp_send.at[1, h],
            recv_sem=dp_recv.at[index, h],
            device_id={"dp": lax.rem(dp + 1, dps)},
            device_id_type=MESH,
        ).wait_recv()

    def in_order(body):
        for d in range(height - 1, -1, -1):
            for way, (z, there) in enumerate(place.by_distance(d)):
                for h in range(HALVES):
                    when(there, lambda z=z, h=h: body(z, h, None if d == 0 else (DOWN, UP)[way]))

    def send_core(z, h, way):
        core_copy(z, 1 - place.x, h).start()

    def send_core_own(z, h, way):
        core_copy(z, place.x, h).start()

    def send_across(z, h, way):
        core_copy(z, 1 - place.x, h).wait_recv()
        span = spans[h]
        total = part_ref[place.at(z, 1 - place.x, place.core), span].astype(f32)
        total = total + core_in[z * COLUMNS + 1 - place.x, span].astype(f32)
        across_out[z, span] = total.astype(jnp.bfloat16)
        across_copy(z, h).start()

    def send_line(z, h, way):
        span = spans[h]
        core_copy(z, place.x, h).wait_recv()
        across_copy(z, h).wait_recv()

        def total():
            own = part_ref[place.at(z, place.x, place.core), span].astype(f32)
            own = own + core_in[z * COLUMNS + place.x, span].astype(f32)
            return own + across_in[z, span].astype(f32)

        if way is None:

            def store(value):
                dp_in[dp, span] = value.astype(jnp.bfloat16)

            def both():
                line_arrive(z, h)
                line_arrive(height, h)
                store(total() + line_in[z, span].astype(f32) + line_in[height, span].astype(f32))

            def above():
                line_arrive(z, h)
                store(total() + line_in[z, span].astype(f32))

            def below():
                line_arrive(height, h)
                store(total() + line_in[height, span].astype(f32))

            pl.when(jnp.logical_and(place.has_up, place.has_down))(both)
            pl.when(jnp.logical_and(place.has_up, jnp.logical_not(place.has_down)))(above)
            pl.when(jnp.logical_and(jnp.logical_not(place.has_up), place.has_down))(below)
            for step in range(1, dps):
                dp_copy(step, h).start()
            return
        if way == DOWN:
            before, slot, target = place.has_up, z, place.down
        else:
            before, target = place.has_down, place.up
            slot = jnp.where(z == place.z + 1, height, z)

        def with_arrival():
            line_arrive(z, h)
            line_out[z, span] = (total() + line_in[z, span].astype(f32)).astype(jnp.bfloat16)

        def alone():
            line_out[z, span] = total().astype(jnp.bfloat16)

        pl.when(before)(with_arrival)
        pl.when(jnp.logical_not(before))(alone)
        line_copy(z, slot, h, target).start()

    in_order(send_core)
    in_order(send_core_own)
    in_order(send_across)
    in_order(send_line)
    for h in range(HALVES):
        for step in range(1, dps):
            dp_arrive(lax.rem(dp + step, dps), h)
        total = dp_in[0, spans[h]].astype(f32)
        for index in range(1, dps):
            total = total + dp_in[index, spans[h]].astype(f32)
        leave(h, spans[h], total)

    def settle(z, h, way):
        core_copy(z, 0, h).wait_send()
        core_copy(z, 1, h).wait_send()
        across_copy(z, h).wait_send()
        if way is not None:
            line_copy(z, 0, h, place.up).wait_send()

    in_order(settle)
    for h in range(HALVES):
        for step in range(1, dps):
            dp_copy(step, h).wait_send()


def scatter_scratch(n, rows, width):
    height = n // (CORES * COLUMNS)
    dps = lax.axis_size("dp")
    sizes = [height * COLUMNS, height, height, height, height + 1, dps]
    sems = [height * COLUMNS] * 2 + [height] * 3 + [height + 1] + [dps] * 2
    return (
        [pltpu.VMEM((size, rows, width), jnp.bfloat16) for size in sizes],
        [pltpu.SemaphoreType.DMA((size, HALVES)) for size in sems],
    )


def gather_scratch(n, pieces):
    return [pltpu.SemaphoreType.DMA((pieces, 4, n)), pltpu.SemaphoreType.DMA((pieces, n))]


def token_pieces(ref):
    rows = ref.shape[1] // HALVES
    return [lambda block, h=h: ref.at[block, pl.ds(h * rows, rows)] for h in range(HALVES)]


def spread_kernel(n, tokens_ref, table_ref, rows_ref, tables_ref, send, recv):
    place = Place(n)
    rows_ref[place.me] = tokens_ref[...]
    tables_ref[place.me] = table_ref[...]
    greet(place, False)
    gather(place, [lambda block: tables_ref.at[block]] + token_pieces(rows_ref), send, recv)


def loss_kernel(n, part_ref, targets_ref, scales_ref, grads_ref, *scratch):
    place = Place(n)
    bufs, sems, (send, recv) = scratch[:6], scratch[6:14], scratch[14:]
    greet(place, True)

    def leave(h, span, total):
        error = total - targets_ref[span, :].astype(jnp.float32)
        grads_ref[place.me, span] = (scales_ref[span, :] * error).astype(jnp.bfloat16)

    scatter(place, part_ref, bufs, sems, leave)
    gather(place, token_pieces(grads_ref), send, recv)


def return_kernel(n, part_ref, out_ref, *scratch):
    place = Place(n)
    bufs, sems = scratch[:6], scratch[6:14]
    greet(place, True)

    def leave(h, span, total):
        out_ref[span, :] = total.astype(jnp.bfloat16)

    scatter(place, part_ref, bufs, sems, leave)


def run(kernel, out_shape, scratch, number, *operands):
    single = not isinstance(out_shape, (list, tuple))
    whole = pl.BlockSpec(memory_space=pltpu.VMEM)
    return pl.pallas_call(
        kernel,
        out_shape=out_shape,
        in_specs=[whole] * len(operands),
        out_specs=whole if single else [whole] * len(out_shape),
        scratch_shapes=scratch,
        compiler_params=pltpu.CompilerParams(
            collective_id=number, has_side_effects=True, vmem_limit_bytes=60 * 2**20
        ),
    )(*operands)


def table_of(routes, route_gates, experts):
    count = routes.shape[0]
    hits = routes[None, :, :] == jnp.arange(experts, dtype=jnp.int32)[:, None, None]
    chosen = jnp.any(hits, 2)
    earlier = jnp.arange(count)[:, None] < jnp.arange(count)[None, :]
    places = jnp.dot(
        chosen.astype(jnp.bfloat16), earlier.astype(jnp.bfloat16), preferred_element_type=jnp.float32
    )
    places = jnp.where(chosen, places, -1.0)
    gates = jnp.sum(jnp.where(hits, route_gates.astype(jnp.float32)[None], 0.0), 2)
    return jnp.concatenate([places, gates], 0).astype(jnp.bfloat16)


def block_dot(left, right, contract):
    return lax.dot_general(
        left, right, ((contract[0], contract[1]), ((0,), (0,))), preferred_element_type=jnp.float32
    ).astype(jnp.bfloat16)


def shards(tokens, routes, route_gates, domains, domain_weight, targets, w_gate, w_up, w_down):
    count, width = tokens.shape
    n = lax.axis_size("expert")
    capacity = max(2, 4 * count * routes.shape[1] // (3 * n))
    bf16, f32 = jnp.bfloat16, jnp.float32
    contract_last = (((1,), (1,)), ((), ()))
    contract_first = (((0,), (0,)), ((), ()))

    table = table_of(routes, route_gates, n)
    rows, tables = run(
        functools.partial(spread_kernel, n),
        [jax.ShapeDtypeStruct((n, count, width), bf16), jax.ShapeDtypeStruct((n, 2 * n, count), bf16)],
        gather_scratch(n, HALVES + 1),
        0,
        tokens,
        table,
    )
    me = lax.axis_index("expert")
    places = lax.dynamic_index_in_dim(tables, me, 1, keepdims=True)
    gates = lax.dynamic_index_in_dim(tables, me + n, 1, keepdims=True)
    matches = places.astype(jnp.int32) == jnp.arange(capacity, dtype=jnp.int32)[None, :, None]
    select = matches.astype(bf16)
    gated = jnp.where(matches, gates, jnp.zeros((), bf16))

    slot_rows = block_dot(select, rows, ((2,), (1,))).reshape(n * capacity, width)
    gate_pre = jnp.dot(slot_rows, w_gate[0], preferred_element_type=f32)
    up_pre = jnp.dot(slot_rows, w_up[0], preferred_element_type=f32)
    hidden = (jax.nn.silu(gate_pre) * up_pre).astype(bf16)
    part = jnp.dot(hidden, w_down[0], preferred_element_type=f32).astype(bf16)
    outs = block_dot(gated, part.reshape(n, capacity, width), ((1,), (1,)))

    picks = domains[:, None] == jnp.arange(domain_weight.shape[0], dtype=jnp.int32)[None, :]
    scales = jnp.sum(jnp.where(picks, domain_weight[None, :], 0.0), 1, keepdims=True)
    bufs, sems = scatter_scratch(n, count, width)
    loss_grads = run(
        functools.partial(loss_kernel, n),
        jax.ShapeDtypeStruct((n, count, width), bf16),
        bufs + sems + gather_scratch(n, HALVES),
        1,
        outs,
        targets,
        scales,
    )

    slot_grads = block_dot(gated, loss_grads, ((2,), (1,))).reshape(n * capacity, width)
    hidden_grad = lax.dot_general(slot_grads, w_down[0], contract_last, preferred_element_type=f32)
    sigma = jax.nn.sigmoid(gate_pre)
    gate_grad = (hidden_grad * up_pre * sigma * (1.0 + gate_pre * (1.0 - sigma))).astype(bf16)
    up_grad = (hidden_grad * gate_pre * sigma).astype(bf16)
    row_part = lax.dot_general(gate_grad, w_gate[0], contract_last, preferred_element_type=f32)
    row_part = row_part + lax.dot_general(up_grad, w_up[0], contract_last, preferred_element_type=f32)
    backs = block_dot(select, row_part.astype(bf16).reshape(n, capacity, width), ((1,), (1,)))
    grad_tokens = run(
        functools.partial(return_kernel, n),
        jax.ShapeDtypeStruct((count, width), bf16),
        bufs + sems,
        2,
        backs,
    )
    grad_down = lax.dot_general(hidden, slot_grads, contract_first, preferred_element_type=f32)
    grad_gate = lax.dot_general(slot_rows, gate_grad, contract_first, preferred_element_type=f32)
    grad_up = lax.dot_general(slot_rows, up_grad, contract_first, preferred_element_type=f32)
    return grad_tokens, grad_gate[None], grad_up[None], grad_down[None]


def solution(mesh):
    return jax.shard_map(
        shards,
        mesh=mesh,
        in_specs=(
            P("expert", None),
            P("expert", None),
            P("expert", None),
            P("expert"),
            P(),
            P("expert", None),
            P("expert", None, "dp"),
            P("expert", None, "dp"),
            P("expert", "dp", None),
        ),
        out_specs=(
            P("expert", None),
            P("expert", None, "dp"),
            P("expert", None, "dp"),
            P("expert", "dp", None),
        ),
        check_vma=False,
    )
```

time: 298 us -> 171 us (0.57); the launches traced: 294 us -> 171 us
  Pallas kernels: 0 us -> 133 us
  blocking collectives: 127 us -> 0 us
  waiting for transfers between devices: 107 us -> 0 us
  between operations: 14.3 us -> 0.82 us
  starting transfers between devices: 10.4 us -> 0 us
    pallas_call x0 -> x3, Pallas kernels: none -> 133 us  [run(): pl.pallas_call(kernel, out_shape=out_shape, in_specs=[whole] * len(operan...]
    all_to_all x2 -> x0, blocking collectives: 108 us -> none  [the longest x1 54.6 us: shards(): lax.all_to_all(send_rows, 'expert', split_axis=0, concat_axis=0, tiled=True)]
    all_to_all x2 -> x0, waiting for transfers between devices: 71.9 us -> none  [the longest x1 40.6 us: shards(): lax.all_to_all(slot_part, 'expert', split_axis=0, concat_axis=0, tiled=True)]
    psum x1 -> x0, waiting for transfers between devices: 35.2 us -> none  [shards(): layer_out = lax.psum(column_out, 'dp')]
    psum x1 -> x0, blocking collectives: 19.3 us -> none  [shards(): grad_tokens = lax.psum(column_input, 'dp')]
    all_to_all x2 -> x0, starting transfers between devices: 10.4 us -> none  [the longest x1 5.24 us: shards(): lax.all_to_all(slot_part, 'expert', split_axis=0, concat_axis=0, tiled=True)]
    dot_general x13 -> x14, matrix products: 28.3 us -> 30.2 us  [the longest x4 12.5 us: block_dot(): lax.dot_general(left, right, ((contract[0], contract[1]), ((0,), (0,))),...]
  transfers between devices with their start and end apart: 3 -> 0, of which waited for: 3 -> 0; matrix products, arithmetic and copies ran while one was open for 4% -> 0% of each run, Pallas kernels for 0% -> 0%
where the time goes in v1:
time: 171 us
  Pallas kernels  133 us (78%)
  matrix products  30.2 us (18%)
  other arithmetic  4.34 us (3%)
  local copies, waits for them, and re-layouts  2.88 us (2%)
    pallas_call x3, Pallas kernels, run(): pl.pallas_call(kernel, out_shape=out_shape, in_specs=[whole] * len(operan...  133 us
    dot_general x4, matrix products, block_dot(): lax.dot_general(left, right, ((contract[0], contract[1]), ((0,), (0,))),...  12.5 us

profile of v1, /device:TPU:0, one launch (start us, length us, event | category | flops | bytes accessed | tf_op | source)
XLA Modules:
  0.0 170.9 jit_solution(10119387249826997440)
XLA Ops:
  0.7 0.8 select_reduce_fusion.1
  1.5 0.7 fusion.22
  2.3 0.7 convert_element_type.35
  3.0 0.7 select_reduce_fusion
  3.7 0.6 pad_maximum_fusion.table_ref
  4.3 0.7 copy.19.scales_ref
  5.1 34.2 %shard_map.120 = (bf16[16,128,1024]{2,1,0:T(8,128)(2,1)}, bf16[16,32,128]{2,1,0:T(8,128)(2,1)}) custom-call(bf16[128,1024]{1,0:T(8,128)(2,1)} %tokens_ref.1, bf16[32,128]{1,0:T(8,128)(2,1)} %pad_maximum_fusion.table_ref), custom_call_target="tpu_custom_call" | custom-call | tf_op jit(solution)/shard_map/pallas_call | solution.py:357
  39.3 0.8 constant_dynamic-slice_fusion
  40.1 3.0 %convolution_convert_fusion.4 = bf16[16,64,1024]{2,1,0:T(8,128)(2,1)S(1)} fusion(bf16[16,128,1024]{2,1,0:T(8,128)(2,1)} %get-tuple-element.7, s32[16,128]{1,0:T(8,128)S(1)} %bitcast.59), kind=kOutput, calls=%fused_computation.9 | convolution fusion | flops 269615104 | bytes 6299648 | tf_op jit(solution)/shard_map/dot_general | solution.py:383
  43.1 1.2 fusion.9
  44.4 2.8 %multiply_convert_fusion.2 = (bf16[1024,512]{1,0:T(8,128)(2,1)S(1)}, f32[1024,512]{1,0:T(8,128)}) fusion(f32[1024,512]{1,0:T(8,128)S(1)} %fusion.9, bf16[1024,1024]{1,0:T(8,128)(2,1)S(1)} %bitcast.55, bf16[1,1024,512]{2,1,0:T(8,128)(2,1)S(1)} %copy-done.3), kind=kOutput, calls=%fused_computation.5 | convolution fusion | flops 1076887552 | bytes 8388608 | tf_op jit(solution)/shard_map/dot_general | solution.py:414
  47.2 1.3 convolution_convert_fusion.3
  48.5 3.2 %convolution_convert_fusion.1.part_ref = bf16[16,128,1024]{2,1,0:T(8,128)(2,1)} fusion(bf16[16,64,1024]{2,1,0:T(8,128)(2,1)S(1)} %bitcast.58, s32[16,128]{1,0:T(8,128)S(1)} %bitcast.60, bf16[16,128]{1,0:T(8,128)(2,1)S(1)} %bitcast.63), kind=kOutput, calls=%fused_computation.2 | convolution fusion | flops 270794752 | bytes 6303744 | tf_op jit(solution)/shard_map/dot_general | solution.py:383
  51.7 63.7 %shard_map.121 = bf16[16,128,1024]{2,1,0:T(8,128)(2,1)} custom-call(bf16[16,128,1024]{2,1,0:T(8,128)(2,1)} %convolution_convert_fusion.1.part_ref, bf16[128,1024]{1,0:T(8,128)(2,1)} %targets_ref.1, f32[128,1]{1,0:T(8,128)} %copy.19.scales_ref), custom_call_target="tpu_custom_call" | custom-call | tf_op jit(solution)/shard_map/pallas_call | solution.py:357
  115.5 3.0 %convolution_convert_fusion.2 = bf16[16,64,1024]{2,1,0:T(8,128)(2,1)S(1)} fusion(bf16[16,128,1024]{2,1,0:T(8,128)(2,1)} %shard_map.121, s32[16,128]{1,0:T(8,128)S(1)} %bitcast.61, bf16[16,128]{1,0:T(8,128)(2,1)S(1)} %bitcast.64), kind=kOutput, calls=%fused_computation.7 | convolution fusion | flops 269746176 | bytes 6303744 | tf_op jit(solution)/shard_map/dot_general | solution.py:383
  118.9 1.9 %multiply_convert_fusion = (bf16[1024,512]{1,0:T(8,128)(2,1)S(1)}, bf16[1024,512]{1,0:T(8,128)(2,1)S(1)}) fusion(f32[1024,512]{1,0:T(8,128)S(1)} %copy-done.8, f32[1024,512]{1,0:T(8,128)S(1)} %copy-done.9, bf16[1024,1024]{1,0:T(8,128)(2,1)S(1)} %bitcast.51, bf16[1,512,1024]{2,1,0:T(8,128)(2,1)S(1)} %copy-done), kind=kOutput, calls=%fused_computation.3 | convolution fusion | flops 1080557568 | bytes 9437184 | tf_op jit(solution)/shard_map/dot_general | solution.py:433
  120.9 2.6 %convolution_bitcast_fusion = f32[1,512,1024]{2,1,0:T(8,128)} fusion(bf16[1024,512]{1,0:T(8,128)(2,1)S(1)} %copy-done.2, bf16[1024,1024]{1,0:T(8,128)(2,1)S(1)} %bitcast.52), kind=kOutput, calls=%fused_computation.10 | convolution fusion | flops 1073741824 | bytes 5242880 | tf_op jit(solution)/shard_map/dot_general | solution.py:447
  123.5 2.6 %convolution_bitcast_fusion.1 = f32[1,1024,512]{2,1,0:T(8,128)} fusion(bf16[1024,1024]{1,0:T(8,128)(2,1)S(1)} %bitcast.56, bf16[1024,512]{1,0:T(8,128)(2,1)S(1)} %get-tuple-element.8), kind=kOutput, calls=%fused_computation.11 | convolution fusion | flops 1073741824 | bytes 5242880 | tf_op jit(solution)/shard_map/dot_general | solution.py:449
  126.1 2.6 %convolution_bitcast_fusion.2 = f32[1,1024,512]{2,1,0:T(8,128)} fusion(bf16[1024,1024]{1,0:T(8,128)(2,1)S(1)} %bitcast.57, bf16[1024,512]{1,0:T(8,128)(2,1)S(1)} %get-tuple-element.9), kind=kOutput, calls=%fused_computation.12 | convolution fusion | flops 1073741824 | bytes 5242880 | tf_op jit(solution)/shard_map/dot_general | solution.py:448
  128.7 1.3 fusion.7
  130.0 1.3 add_convert_fusion
  131.3 3.2 %convolution_convert_fusion.part_ref = bf16[16,128,1024]{2,1,0:T(8,128)(2,1)} fusion(bf16[16,64,1024]{2,1,0:T(8,128)(2,1)S(1)} %bitcast.53, s32[16,128]{1,0:T(8,128)S(1)} %bitcast.62), kind=kOutput, calls=%fused_computation.1 | convolution fusion | flops 270663680 | bytes 6299648 | tf_op jit(solution)/shard_map/dot_general | solution.py:383
  134.5 34.7 %shard_map.122 = bf16[128,1024]{1,0:T(8,128)(2,1)} custom-call(bf16[16,128,1024]{2,1,0:T(8,128)(2,1)} %convolution_convert_fusion.part_ref), custom_call_target="tpu_custom_call" | custom-call | tf_op jit(solution)/shard_map/pallas_call | solution.py:357
  169.3 1.7 copy.24
  (22 shorter events, 0.6 us)
Async XLA Ops:
  0.6 46.5 %copy-start = (bf16[1,512,1024]{2,1,0:T(8,128)(2,1)S(1)}, bf16[1,512,1024]{2,1,0:T(8,128)(2,1)}, u32[]{:S(2)}) copy-start(bf16[1,512,1024]{2,1,0:T(8,128)(2,1)} %param.17) | copy-start | bytes 3145732
  40.1 3.0 %copy-start.5 = (bf16[1,1024,512]{2,1,0:T(8,128)(2,1)S(1)}, bf16[1,1024,512]{2,1,0:T(8,128)(2,1)}, u32[]{:S(2)}) copy-start(bf16[1,1024,512]{2,1,0:T(8,128)(2,1)} %param.15) | copy-start | bytes 3145732
  43.1 1.3 copy-start.3
  44.4 2.8 %copy-start.7 = (f32[1024,512]{1,0:T(8,128)}, f32[1024,512]{1,0:T(8,128)S(1)}, u32[]{:S(2)}) copy-start(f32[1024,512]{1,0:T(8,128)S(1)} %fusion.9) | copy-start | bytes 6291460
  47.2 1.3 copy-start.1
  115.4 3.1 %copy-start.8 = (f32[1024,512]{1,0:T(8,128)S(1)}, f32[1024,512]{1,0:T(8,128)}, u32[]{:S(2)}) copy-start(f32[1024,512]{1,0:T(8,128)} %copy-done.7) | copy-start | bytes 6291460
  115.4 3.5 %copy-start.9 = (f32[1024,512]{1,0:T(8,128)S(1)}, f32[1024,512]{1,0:T(8,128)}, u32[]{:S(2)}) copy-start(f32[1024,512]{1,0:T(8,128)} %get-tuple-element.13) | copy-start | bytes 6291460
  118.9 2.0 %copy-start.2 = (bf16[1024,512]{1,0:T(8,128)(2,1)S(1)}, bf16[1024,512]{1,0:T(8,128)(2,1)}, u32[]{:S(2)}) copy-start(bf16[1024,512]{1,0:T(8,128)(2,1)} %copy-done.1) | copy-start | bytes 3145732
  126.1 2.6 %copy-start.6 = (bf16[1,1024,512]{2,1,0:T(8,128)(2,1)S(1)}, bf16[1,1024,512]{2,1,0:T(8,128)(2,1)}, u32[]{:S(2)}) copy-start(bf16[1,1024,512]{2,1,0:T(8,128)(2,1)} %param.15) | copy-start | bytes 3145732
  128.7 1.3 copy-start.4

commit v2 on v1

v2 whole, which is shorter than its diff:
```python
import functools

import jax
import jax.numpy as jnp
from jax import lax
from jax.experimental import pallas as pl
from jax.experimental.pallas import tpu as pltpu
from jax.sharding import PartitionSpec as P

MESH = pl.DeviceIdType.MESH
CORES = 2
COLUMNS = 2
PIECES = 4
UP, DOWN, ACROSS, SIBLING, PARTNER = range(5)


class Place:
    def __init__(self, n):
        self.n = n
        self.height = n // (CORES * COLUMNS)
        self.me = lax.axis_index("expert")
        self.core = lax.rem(self.me, CORES)
        self.x = lax.rem(self.me // CORES, COLUMNS)
        self.z = self.me // (CORES * COLUMNS)
        self.up = self.me + CORES * COLUMNS
        self.down = self.me - CORES * COLUMNS
        self.has_up = self.z + 1 < self.height
        self.has_down = self.z > 0
        self.parity = lax.rem(lax.axis_index("dp"), 2)
        self.partner = lax.axis_index("dp") + 1 - 2 * self.parity
        self.across = self.at(self.z, 1 - self.x, self.core)
        self.sibling = self.at(self.z, self.x, 1 - self.core)

    def at(self, z, x, core):
        return (z * COLUMNS + x) * CORES + core

    def by_distance(self, d):
        if d == 0:
            return [(self.z, None)]
        return [(self.z - d, self.z - d >= 0), (self.z + d, self.z + d < self.height)]


def when(condition, body):
    if condition is None:
        body()
    else:
        pl.when(condition)(body)


def greet(place):
    barrier = pltpu.get_barrier_semaphore()

    def signal(target):
        pl.semaphore_signal(barrier, inc=1, device_id=target, device_id_type=MESH)

    pl.when(place.has_up)(lambda: signal({"expert": place.up}))
    pl.when(place.has_down)(lambda: signal({"expert": place.down}))
    signal({"expert": place.across})
    signal({"expert": place.sibling})
    count = 2 + place.has_up.astype(jnp.int32) + place.has_down.astype(jnp.int32)
    dps = lax.axis_size("dp")
    for step in range(1, dps):
        signal({"dp": lax.rem(lax.axis_index("dp") + step, dps)})
    count = count + (dps - 1)
    pl.semaphore_wait(barrier, count)


class Gather:
    def __init__(self, place, pieces, extra, send, recv):
        self.place, self.pieces, self.extra, self.send, self.recv = place, pieces, extra, send, recv

    def copy(self, piece, block, link):
        place = self.place
        view = self.extra(block) if piece is None else self.pieces(block, piece)
        number = PIECES if piece is None else piece
        target = {
            UP: {"expert": place.up},
            DOWN: {"expert": place.down},
            ACROSS: {"expert": place.across},
            SIBLING: {"expert": place.sibling},
            PARTNER: {"dp": place.partner},
        }[link]
        return pltpu.make_async_remote_copy(
            src_ref=view,
            dst_ref=view,
            send_sem=self.send.at[number, link, block],
            recv_sem=self.recv.at[number, block],
            device_id=target,
            device_id_type=MESH,
        )

    def arrive(self, piece, block):
        self.copy(piece, block, SIBLING).wait_recv()

    def mine(self, z):
        return self.place.at(z, self.place.x, self.place.core)

    def other(self, z):
        return self.place.at(z, 1 - self.place.x, self.place.core)

    def line_pieces(self):
        found = [] if self.extra is None else [(None, True)]
        for k in range(PIECES // 2):
            found += [(2 * k + self.place.parity, True), (2 * k + 1 - self.place.parity, False)]
        return found

    def begin(self, piece, shared):
        place, me = self.place, self.place.me
        pl.when(place.has_up)(lambda: self.copy(piece, me, UP).start())
        pl.when(place.has_down)(lambda: self.copy(piece, me, DOWN).start())
        if shared:
            self.copy(piece, me, ACROSS).start()
        self.copy(piece, me, SIBLING).start()

    def line_step(self, d, piece, shared):
        place = self.place
        for (z, there), onward, open_ in zip(
            place.by_distance(d), (UP, DOWN), (place.has_up, place.has_down)
        ):

            def body(z=z, onward=onward, open_=open_):
                self.arrive(piece, self.mine(z))
                pl.when(open_)(lambda: self.copy(piece, self.mine(z), onward).start())
                if shared:
                    self.copy(piece, self.mine(z), ACROSS).start()
                self.copy(piece, self.mine(z), SIBLING).start()

            when(there, body)

    def across_step(self, d, piece, shared):
        for z, there in self.place.by_distance(d):

            def body(z=z):
                self.arrive(piece, self.other(z))
                if shared and piece is not None:
                    self.copy(piece, self.other(z), PARTNER).start()
                self.copy(piece, self.other(z), SIBLING).start()

            when(there, body)

    def run(self):
        height = self.place.height
        for d in range(1, height + 2):
            for piece, shared in self.line_pieces():
                if d < height:
                    self.line_step(d, piece, shared)
                if shared and d <= height:
                    self.across_step(d - 1, piece, True)
                if not shared and d >= 2:
                    self.across_step(d - 2, piece, False)
        self.finish()

    def finish(self):
        place = self.place
        for z in range(place.height):
            for piece, shared in self.line_pieces():
                for x in range(COLUMNS):
                    self.arrive(piece, place.at(z, x, 1 - place.core))
                self.copy(piece, self.mine(z), SIBLING).wait_send()
                self.copy(piece, self.other(z), SIBLING).wait_send()
                if shared:
                    self.copy(piece, self.mine(z), ACROSS).wait_send()
                    if piece is not None:
                        self.copy(piece, self.other(z), PARTNER).wait_send()
                pl.when(jnp.logical_and(place.has_up, z <= place.z))(
                    lambda: self.copy(piece, self.mine(z), UP).wait_send()
                )
                pl.when(jnp.logical_and(place.has_down, z >= place.z))(
                    lambda: self.copy(piece, self.mine(z), DOWN).wait_send()
                )


def scatter(place, part_ref, bufs, sems, leave):
    core_in, partner_in, across_in, line_in, dp_in = bufs
    core_sems, partner_sems, across_sems, line_sems, dp_sems = [
        (sems[2 * i], sems[2 * i + 1]) for i in range(5)
    ]
    height = place.height
    rows = part_ref.shape[1] // PIECES
    dps = lax.axis_size("dp")
    dp = lax.axis_index("dp")
    f32 = jnp.float32

    def span_of(h):
        return pl.ds(pl.multiple_of(h * rows, rows), rows)

    def remote(source, target, pair, source_index, target_index, h, device):
        return pltpu.make_async_remote_copy(
            src_ref=source.at[source_index, span_of(h)],
            dst_ref=target.at[target_index, span_of(h)],
            send_sem=pair[0].at[source_index, h],
            recv_sem=pair[1].at[target_index, h],
            device_id=device,
            device_id_type=MESH,
        )

    def core_copy(z, x, h):
        spot = z * COLUMNS + x
        return pltpu.make_async_remote_copy(
            src_ref=part_ref.at[place.at(z, x, 1 - place.core), span_of(h)],
            dst_ref=core_in.at[spot, span_of(h)],
            send_sem=core_sems[0].at[spot, h],
            recv_sem=core_sems[1].at[spot, h],
            device_id={"expert": place.sibling},
            device_id_type=MESH,
        )

    def spot_of(z, x):
        return z * COLUMNS + x

    def partner_copy(z, h):
        return remote(
            core_in, partner_in, partner_sems, spot_of(z, 1 - place.x), z, h, {"dp": place.partner}
        )

    def across_copy(z, h):
        return remote(
            core_in, across_in, across_sems, spot_of(z, 1 - place.x), z, h, {"expert": place.across}
        )

    def line_copy(z, slot, h, target):
        return remote(
            core_in, line_in, line_sems, spot_of(z, place.x), slot, h, {"expert": target}
        )

    def line_arrive(slot, h):
        line_copy(0, slot, h, place.up).wait_recv()

    def dp_copy(step, h):
        return pltpu.make_async_remote_copy(
            src_ref=dp_in.at[dp, span_of(h)],
            dst_ref=dp_in.at[dp, span_of(h)],
            send_sem=dp_sems[0].at[step, h],
            recv_sem=dp_sems[1].at[dp, h],
            device_id={"dp": lax.rem(dp + step, dps)},
            device_id_type=MESH,
        )

    def dp_arrive(index, h):
        pltpu.make_async_remote_copy(
            src_ref=dp_in.at[dp, span_of(h)],
            dst_ref=dp_in.at[index, span_of(h)],
            send_sem=dp_sems[0].at[1, h],
            recv_sem=dp_sems[1].at[index, h],
            device_id={"dp": lax.rem(dp + 1, dps)},
            device_id_type=MESH,
        ).wait_recv()

    own_half = [2 * k + place.parity for k in range(PIECES // 2)]
    their_half = [2 * k + 1 - place.parity for k in range(PIECES // 2)]

    def planes(d, halves, body):
        for way, (z, there) in enumerate(place.by_distance(d)):
            for h, shared in halves:
                when(there, lambda z=z, h=h: body(z, h, shared, None if d == 0 else (DOWN, UP)[way]))

    both_halves = [(h, True) for h in own_half] + [(h, False) for h in their_half]

    def send_core(z, h, shared, way):
        core_copy(z, 1 - place.x, h).start()

    def send_core_own(z, h, shared, way):
        core_copy(z, place.x, h).start()

    def add_core(z, x, h):
        total = part_ref[place.at(z, x, place.core), span_of(h)].astype(f32)
        return total + core_in[spot_of(z, x), span_of(h)].astype(f32)

    def send_partner(z, h, shared, way):
        core_copy(z, 1 - place.x, h).wait_recv()
        core_in[spot_of(z, 1 - place.x), span_of(h)] = add_core(z, 1 - place.x, h).astype(jnp.bfloat16)
        partner_copy(z, h).start()

    def send_across(z, h, shared, way):
        core_copy(z, 1 - place.x, h).wait_recv()
        partner_copy(z, h).wait_recv()
        total = add_core(z, 1 - place.x, h) + partner_in[z, span_of(h)].astype(f32)
        core_in[spot_of(z, 1 - place.x), span_of(h)] = total.astype(jnp.bfloat16)
        across_copy(z, h).start()

    def send_line(z, h, shared, way):
        span = span_of(h)
        core_copy(z, place.x, h).wait_recv()
        if shared:
            across_copy(z, h).wait_recv()

        def total():
            own = add_core(z, place.x, h)
            return own + across_in[z, span].astype(f32) if shared else own

        if way is None:

            def store(value):
                dp_in[dp, span] = value.astype(jnp.bfloat16)

            def both():
                line_arrive(z, h)
                line_arrive(height, h)
                store(total() + line_in[z, span].astype(f32) + line_in[height, span].astype(f32))

            def above():
                line_arrive(z, h)
                store(total() + line_in[z, span].astype(f32))

            def below():
                line_arrive(height, h)
                store(total() + line_in[height, span].astype(f32))

            pl.when(jnp.logical_and(place.has_up, place.has_down))(both)
            pl.when(jnp.logical_and(place.has_up, jnp.logical_not(place.has_down)))(above)
            pl.when(jnp.logical_and(jnp.logical_not(place.has_up), place.has_down))(below)
            for step in range(1, dps):
                dp_copy(step, h).start()
            return
        if way == DOWN:
            before, slot, target = place.has_up, z, place.down
        else:
            before, target = place.has_down, place.up
            slot = jnp.where(z == place.z + 1, height, z)

        def store_line(value):
            core_in[spot_of(z, place.x), span] = value.astype(jnp.bfloat16)

        def with_arrival():
            line_arrive(z, h)
            store_line(total() + line_in[z, span].astype(f32))

        pl.when(before)(with_arrival)
        pl.when(jnp.logical_not(before))(lambda: store_line(total()))
        line_copy(z, slot, h, target).start()

    far_first = range(height - 1, -1, -1)
    for d in far_first:
        planes(d, both_halves[::-1], send_core)
    for d in far_first:
        planes(d, both_halves, send_core_own)
    for d in far_first:
        planes(d, both_halves[PIECES // 2 :], send_partner)
    for d in far_first:
        planes(d, both_halves[: PIECES // 2], send_across)
        if d + 1 < height:
            planes(d + 1, both_halves[::-1], send_line)
    planes(0, both_halves[::-1], send_line)

    for h, shared in both_halves[::-1]:
        for step in range(1, dps):
            dp_arrive(lax.rem(dp + step, dps), h)
        total = dp_in[0, span_of(h)].astype(f32)
        for index in range(1, dps):
            total = total + dp_in[index, span_of(h)].astype(f32)
        leave(h, shared, span_of(h), total)

    def settle(z, h, shared, way):
        core_copy(z, 0, h).wait_send()
        core_copy(z, 1, h).wait_send()
        (across_copy if shared else partner_copy)(z, h).wait_send()
        if way is not None:
            line_copy(z, 0, h, place.up).wait_send()

    def finish():
        for d in far_first:
            planes(d, both_halves, settle)
        for h in range(PIECES):
            for step in range(1, dps):
                dp_copy(step, h).wait_send()

    return finish


def scatter_scratch(n, rows, width):
    height = n // (CORES * COLUMNS)
    dps = lax.axis_size("dp")
    sizes = [height * COLUMNS, height, height, height + 1, dps]
    return (
        [pltpu.VMEM((size, rows, width), jnp.bfloat16) for size in sizes],
        [pltpu.SemaphoreType.DMA((count, PIECES)) for size in sizes for count in (max(sizes), size)],
    )


def gather_scratch(n):
    return [pltpu.SemaphoreType.DMA((PIECES + 1, 5, n)), pltpu.SemaphoreType.DMA((PIECES + 1, n))]


def token_pieces(ref):
    rows = ref.shape[1] // PIECES
    return lambda block, h: ref.at[block, pl.ds(pl.multiple_of(h * rows, rows), rows)]


def spread_kernel(n, tokens_ref, table_ref, rows_ref, tables_ref, send, recv):
    place = Place(n)
    rows_ref[place.me] = tokens_ref[...]
    tables_ref[place.me] = table_ref[...]
    greet(place)
    spread = Gather(place, token_pieces(rows_ref), lambda block: tables_ref.at[block], send, recv)
    for piece, shared in spread.line_pieces():
        spread.begin(piece, shared)
    spread.run()


def loss_kernel(n, part_ref, targets_ref, scales_ref, grads_ref, *scratch):
    place = Place(n)
    bufs, sems, (send, recv) = scratch[:5], scratch[5:15], scratch[15:]
    greet(place)
    spread = Gather(place, token_pieces(grads_ref), None, send, recv)

    def leave(h, shared, span, total):
        error = total - targets_ref[span, :].astype(jnp.float32)
        grads_ref[place.me, span] = (scales_ref[span, :] * error).astype(jnp.bfloat16)
        spread.begin(h, shared)

    finish = scatter(place, part_ref, bufs, sems, leave)
    spread.run()
    finish()


def return_kernel(n, part_ref, out_ref, *scratch):
    place = Place(n)
    bufs, sems = scratch[:5], scratch[5:15]
    greet(place)

    def leave(h, shared, span, total):
        out_ref[span, :] = total.astype(jnp.bfloat16)

    scatter(place, part_ref, bufs, sems, leave)()


def run(kernel, out_shape, scratch, number, *operands):
    single = not isinstance(out_shape, (list, tuple))
    whole = pl.BlockSpec(memory_space=pltpu.VMEM)
    return pl.pallas_call(
        kernel,
        out_shape=out_shape,
        in_specs=[whole] * len(operands),
        out_specs=whole if single else [whole] * len(out_shape),
        scratch_shapes=scratch,
        compiler_params=pltpu.CompilerParams(
            collective_id=number, has_side_effects=True, vmem_limit_bytes=60 * 2**20
        ),
    )(*operands)


def table_of(routes, route_gates, experts):
    count = routes.shape[0]
    hits = routes[None, :, :] == jnp.arange(experts, dtype=jnp.int32)[:, None, None]
    chosen = jnp.any(hits, 2)
    earlier = jnp.arange(count)[:, None] < jnp.arange(count)[None, :]
    places = jnp.dot(
        chosen.astype(jnp.bfloat16), earlier.astype(jnp.bfloat16), preferred_element_type=jnp.float32
    )
    places = jnp.where(chosen, places, -1.0)
    gates = jnp.sum(jnp.where(hits, route_gates.astype(jnp.float32)[None], 0.0), 2)
    return jnp.concatenate([places, gates], 0).astype(jnp.bfloat16)


def block_dot(left, right, contract):
    return lax.dot_general(
        left, right, ((contract[0], contract[1]), ((0,), (0,))), preferred_element_type=jnp.float32
    ).astype(jnp.bfloat16)


def shards(tokens, routes, route_gates, domains, domain_weight, targets, w_gate, w_up, w_down):
    count, width = tokens.shape
    n = lax.axis_size("expert")
    capacity = max(2, 4 * count * routes.shape[1] // (3 * n))
    bf16, f32 = jnp.bfloat16, jnp.float32
    contract_last = (((1,), (1,)), ((), ()))
    contract_first = (((0,), (0,)), ((), ()))

    table = table_of(routes, route_gates, n)
    rows, tables = run(
        functools.partial(spread_kernel, n),
        [jax.ShapeDtypeStruct((n, count, width), bf16), jax.ShapeDtypeStruct((n, 2 * n, count), bf16)],
        gather_scratch(n),
        0,
        tokens,
        table,
    )
    me = lax.axis_index("expert")
    places = lax.dynamic_index_in_dim(tables, me, 1, keepdims=True)
    gates = lax.dynamic_index_in_dim(tables, me + n, 1, keepdims=True)
    matches = places.astype(jnp.int32) == jnp.arange(capacity, dtype=jnp.int32)[None, :, None]
    select = matches.astype(bf16)
    gated = jnp.where(matches, gates, jnp.zeros((), bf16))

    slot_rows = block_dot(select, rows, ((2,), (1,))).reshape(n * capacity, width)
    gate_pre = jnp.dot(slot_rows, w_gate[0], preferred_element_type=f32)
    up_pre = jnp.dot(slot_rows, w_up[0], preferred_element_type=f32)
    hidden = (jax.nn.silu(gate_pre) * up_pre).astype(bf16)
    part = jnp.dot(hidden, w_down[0], preferred_element_type=f32).astype(bf16)
    outs = block_dot(gated, part.reshape(n, capacity, width), ((1,), (1,)))

    picks = domains[:, None] == jnp.arange(domain_weight.shape[0], dtype=jnp.int32)[None, :]
    scales = jnp.sum(jnp.where(picks, domain_weight[None, :], 0.0), 1, keepdims=True)
    bufs, sems = scatter_scratch(n, count, width)
    loss_grads = run(
        functools.partial(loss_kernel, n),
        jax.ShapeDtypeStruct((n, count, width), bf16),
        bufs + sems + gather_scratch(n),
        1,
        outs,
        targets,
        scales,
    )

    slot_grads = block_dot(gated, loss_grads, ((2,), (1,))).reshape(n * capacity, width)
    hidden_grad = lax.dot_general(slot_grads, w_down[0], contract_last, preferred_element_type=f32)
    sigma = jax.nn.sigmoid(gate_pre)
    gate_grad = (hidden_grad * up_pre * sigma * (1.0 + gate_pre * (1.0 - sigma))).astype(bf16)
    up_grad = (hidden_grad * gate_pre * sigma).astype(bf16)
    row_part = lax.dot_general(gate_grad, w_gate[0], contract_last, preferred_element_type=f32)
    row_part = row_part + lax.dot_general(up_grad, w_up[0], contract_last, preferred_element_type=f32)
    backs = block_dot(select, row_part.astype(bf16).reshape(n, capacity, width), ((1,), (1,)))
    grad_tokens = run(
        functools.partial(return_kernel, n),
        jax.ShapeDtypeStruct((count, width), bf16),
        bufs + sems,
        2,
        backs,
    )
    grad_down = lax.dot_general(hidden, slot_grads, contract_first, preferred_element_type=f32)
    grad_gate = lax.dot_general(slot_rows, gate_grad, contract_first, preferred_element_type=f32)
    grad_up = lax.dot_general(slot_rows, up_grad, contract_first, preferred_element_type=f32)
    return grad_tokens, grad_gate[None], grad_up[None], grad_down[None]


def solution(mesh):
    return jax.shard_map(
        shards,
        mesh=mesh,
        in_specs=(
            P("expert", None),
            P("expert", None),
            P("expert", None),
            P("expert"),
            P(),
            P("expert", None),
            P("expert", None, "dp"),
            P("expert", None, "dp"),
            P("expert", "dp", None),
        ),
        out_specs=(
            P("expert", None),
            P("expert", None, "dp"),
            P("expert", None, "dp"),
            P("expert", "dp", None),
        ),
        check_vma=False,
    )
```

time: 171 us -> 179 us (1.047)
  Pallas kernels: 133 us -> 139 us
    pallas_call x3, Pallas kernels: 133 us -> 139 us  [run(): pl.pallas_call(kernel, out_shape=out_shape, in_specs=[whole] * len(operan...]
where the time goes in v2:
time: 179 us; the launch traced here: 178 us
  Pallas kernels  139 us (78%)
  matrix products  30.2 us (17%)
  other arithmetic  4.34 us (2%)
  local copies, waits for them, and re-layouts  2.87 us (2%)
    pallas_call x3, Pallas kernels, run(): pl.pallas_call(kernel, out_shape=out_shape, in_specs=[whole] * len(operan...  139 us
    dot_general x4, matrix products, block_dot(): lax.dot_general(left, right, ((contract[0], contract[1]), ((0,), (0,))),...  12.5 us

profile of v2, /device:TPU:0, one launch (start us, length us, event | category | flops | bytes accessed | tf_op | source)
XLA Modules:
  0.0 177.7 jit_solution(5595298505882186842)
XLA Ops:
  0.7 0.8 select_reduce_fusion.1
  1.5 0.7 fusion.22
  2.3 0.7 convert_element_type.35
  3.0 0.7 select_reduce_fusion
  3.7 0.6 pad_maximum_fusion.table_ref
  4.3 0.7 copy.19.scales_ref
  5.1 37.4 %shard_map.120 = (bf16[16,128,1024]{2,1,0:T(8,128)(2,1)}, bf16[16,32,128]{2,1,0:T(8,128)(2,1)}) custom-call(bf16[128,1024]{1,0:T(8,128)(2,1)} %tokens_ref.1, bf16[32,128]{1,0:T(8,128)(2,1)} %pad_maximum_fusion.table_ref), custom_call_target="tpu_custom_call" | custom-call | tf_op jit(solution)/shard_map/pallas_call | solution.py:430
  42.4 0.8 constant_dynamic-slice_fusion
  43.3 3.0 %convolution_convert_fusion.4 = bf16[16,64,1024]{2,1,0:T(8,128)(2,1)S(1)} fusion(bf16[16,128,1024]{2,1,0:T(8,128)(2,1)} %get-tuple-element.7, s32[16,128]{1,0:T(8,128)S(1)} %bitcast.59), kind=kOutput, calls=%fused_computation.9 | convolution fusion | flops 269615104 | bytes 6299648 | tf_op jit(solution)/shard_map/dot_general | solution.py:456
  46.3 1.2 fusion.9
  47.5 2.8 %multiply_convert_fusion.2 = (bf16[1024,512]{1,0:T(8,128)(2,1)S(1)}, f32[1024,512]{1,0:T(8,128)}) fusion(f32[1024,512]{1,0:T(8,128)S(1)} %fusion.9, bf16[1024,1024]{1,0:T(8,128)(2,1)S(1)} %bitcast.55, bf16[1,1024,512]{2,1,0:T(8,128)(2,1)S(1)} %copy-done.3), kind=kOutput, calls=%fused_computation.5 | convolution fusion | flops 1076887552 | bytes 8388608 | tf_op jit(solution)/shard_map/dot_general | solution.py:487
  50.3 1.3 convolution_convert_fusion.3
  51.6 3.2 %convolution_convert_fusion.1.part_ref = bf16[16,128,1024]{2,1,0:T(8,128)(2,1)} fusion(bf16[16,64,1024]{2,1,0:T(8,128)(2,1)S(1)} %bitcast.58, s32[16,128]{1,0:T(8,128)S(1)} %bitcast.60, bf16[16,128]{1,0:T(8,128)(2,1)S(1)} %bitcast.63), kind=kOutput, calls=%fused_computation.2 | convolution fusion | flops 270794752 | bytes 6303744 | tf_op jit(solution)/shard_map/dot_general | solution.py:456
  54.8 67.4 %shard_map.121 = bf16[16,128,1024]{2,1,0:T(8,128)(2,1)} custom-call(bf16[16,128,1024]{2,1,0:T(8,128)(2,1)} %convolution_convert_fusion.1.part_ref, bf16[128,1024]{1,0:T(8,128)(2,1)} %targets_ref.1, f32[128,1]{1,0:T(8,128)} %copy.19.scales_ref), custom_call_target="tpu_custom_call" | custom-call | tf_op jit(solution)/shard_map/pallas_call | solution.py:430
  122.3 3.0 %convolution_convert_fusion.2 = bf16[16,64,1024]{2,1,0:T(8,128)(2,1)S(1)} fusion(bf16[16,128,1024]{2,1,0:T(8,128)(2,1)} %shard_map.121, s32[16,128]{1,0:T(8,128)S(1)} %bitcast.61, bf16[16,128]{1,0:T(8,128)(2,1)S(1)} %bitcast.64), kind=kOutput, calls=%fused_computation.7 | convolution fusion | flops 269746176 | bytes 6303744 | tf_op jit(solution)/shard_map/dot_general | solution.py:456
  125.7 1.9 %multiply_convert_fusion = (bf16[1024,512]{1,0:T(8,128)(2,1)S(1)}, bf16[1024,512]{1,0:T(8,128)(2,1)S(1)}) fusion(f32[1024,512]{1,0:T(8,128)S(1)} %copy-done.8, f32[1024,512]{1,0:T(8,128)S(1)} %copy-done.9, bf16[1024,1024]{1,0:T(8,128)(2,1)S(1)} %bitcast.51, bf16[1,512,1024]{2,1,0:T(8,128)(2,1)S(1)} %copy-done), kind=kOutput, calls=%fused_computation.3 | convolution fusion | flops 1080557568 | bytes 9437184 | tf_op jit(solution)/shard_map/dot_general | solution.py:506
  127.7 2.6 %convolution_bitcast_fusion = f32[1,512,1024]{2,1,0:T(8,128)} fusion(bf16[1024,512]{1,0:T(8,128)(2,1)S(1)} %copy-done.2, bf16[1024,1024]{1,0:T(8,128)(2,1)S(1)} %bitcast.52), kind=kOutput, calls=%fused_computation.10 | convolution fusion | flops 1073741824 | bytes 5242880 | tf_op jit(solution)/shard_map/dot_general | solution.py:520
  130.3 2.6 %convolution_bitcast_fusion.1 = f32[1,1024,512]{2,1,0:T(8,128)} fusion(bf16[1024,1024]{1,0:T(8,128)(2,1)S(1)} %bitcast.56, bf16[1024,512]{1,0:T(8,128)(2,1)S(1)} %get-tuple-element.8), kind=kOutput, calls=%fused_computation.11 | convolution fusion | flops 1073741824 | bytes 5242880 | tf_op jit(solution)/shard_map/dot_general | solution.py:522
  132.9 2.6 %convolution_bitcast_fusion.2 = f32[1,1024,512]{2,1,0:T(8,128)} fusion(bf16[1024,1024]{1,0:T(8,128)(2,1)S(1)} %bitcast.57, bf16[1024,512]{1,0:T(8,128)(2,1)S(1)} %get-tuple-element.9), kind=kOutput, calls=%fused_computation.12 | convolution fusion | flops 1073741824 | bytes 5242880 | tf_op jit(solution)/shard_map/dot_general | solution.py:521
  135.5 1.3 fusion.7
  136.8 1.3 add_convert_fusion
  138.1 3.2 %convolution_convert_fusion.part_ref = bf16[16,128,1024]{2,1,0:T(8,128)(2,1)} fusion(bf16[16,64,1024]{2,1,0:T(8,128)(2,1)S(1)} %bitcast.53, s32[16,128]{1,0:T(8,128)S(1)} %bitcast.62), kind=kOutput, calls=%fused_computation.1 | convolution fusion | flops 270663680 | bytes 6299648 | tf_op jit(solution)/shard_map/dot_general | solution.py:456
  141.4 34.7 %shard_map.122 = bf16[128,1024]{1,0:T(8,128)(2,1)} custom-call(bf16[16,128,1024]{2,1,0:T(8,128)(2,1)} %convolution_convert_fusion.part_ref), custom_call_target="tpu_custom_call" | custom-call | tf_op jit(solution)/shard_map/pallas_call | solution.py:430
  176.1 1.7 copy.24
  (22 shorter events, 0.6 us)
Async XLA Ops:
  0.6 49.7 %copy-start = (bf16[1,512,1024]{2,1,0:T(8,128)(2,1)S(1)}, bf16[1,512,1024]{2,1,0:T(8,128)(2,1)}, u32[]{:S(2)}) copy-start(bf16[1,512,1024]{2,1,0:T(8,128)(2,1)} %param.17) | copy-start | bytes 3145732
  43.3 3.0 %copy-start.5 = (bf16[1,1024,512]{2,1,0:T(8,128)(2,1)S(1)}, bf16[1,1024,512]{2,1,0:T(8,128)(2,1)}, u32[]{:S(2)}) copy-start(bf16[1,1024,512]{2,1,0:T(8,128)(2,1)} %param.15) | copy-start | bytes 3145732
  46.3 1.3 copy-start.3
  47.5 2.8 %copy-start.7 = (f32[1024,512]{1,0:T(8,128)}, f32[1024,512]{1,0:T(8,128)S(1)}, u32[]{:S(2)}) copy-start(f32[1024,512]{1,0:T(8,128)S(1)} %fusion.9) | copy-start | bytes 6291460
  50.3 1.3 copy-start.1
  122.2 3.1 %copy-start.8 = (f32[1024,512]{1,0:T(8,128)S(1)}, f32[1024,512]{1,0:T(8,128)}, u32[]{:S(2)}) copy-start(f32[1024,512]{1,0:T(8,128)} %copy-done.7) | copy-start | bytes 6291460
  122.3 3.5 %copy-start.9 = (f32[1024,512]{1,0:T(8,128)S(1)}, f32[1024,512]{1,0:T(8,128)}, u32[]{:S(2)}) copy-start(f32[1024,512]{1,0:T(8,128)} %get-tuple-element.13) | copy-start | bytes 6291460
  125.7 1.9 %copy-start.2 = (bf16[1024,512]{1,0:T(8,128)(2,1)S(1)}, bf16[1024,512]{1,0:T(8,128)(2,1)}, u32[]{:S(2)}) copy-start(bf16[1024,512]{1,0:T(8,128)(2,1)} %copy-done.1) | copy-start | bytes 3145732
  132.9 2.6 %copy-start.6 = (bf16[1,1024,512]{2,1,0:T(8,128)(2,1)S(1)}, bf16[1,1024,512]{2,1,0:T(8,128)(2,1)}, u32[]{:S(2)}) copy-start(bf16[1,1024,512]{2,1,0:T(8,128)(2,1)} %param.15) | copy-start | bytes 3145732
  135.5 1.3 copy-start.4

commit v3 on v1

--- a/solution.py
+++ b/solution.py
@@ -11,6 +11,7 @@
 CORES = 2
 COLUMNS = 2
 HALVES = 2
+LAG = 4
 UP, DOWN, ACROSS, SIBLING = range(4)
 
 
@@ -45,7 +46,7 @@
         pl.when(condition)(body)
 
 
-def greet(place, dp_too):
+def greet(place):
     barrier = pltpu.get_barrier_semaphore()
 
     def signal(target):
@@ -56,87 +57,104 @@
     signal({"expert": place.across})
     signal({"expert": place.sibling})
     count = 2 + place.has_up.astype(jnp.int32) + place.has_down.astype(jnp.int32)
-    if dp_too:
-        dps = lax.axis_size("dp")
-        mine = lax.axis_index("dp")
-        for step in range(1, dps):
-            signal({"dp": lax.rem(mine + step, dps)})
-        count = count + (dps - 1)
+    dps = lax.axis_size("dp")
+    for step in range(1, dps):
+        signal({"dp": lax.rem(lax.axis_index("dp") + step, dps)})
+    count = count + (dps - 1)
     pl.semaphore_wait(barrier, count)
 
 
-def gather(place, pieces, send, recv):
-    links = {
-        UP: (place.up, place.has_up),
-        DOWN: (place.down, place.has_down),
-        ACROSS: (place.across, None),
-        SIBLING: (place.sibling, None),
-    }
-
-    def copy(piece, block, link):
-        view = pieces[piece](block)
+class Gather:
+    def __init__(self, place, pieces, send, recv):
+        self.place, self.pieces, self.send, self.recv = place, pieces, send, recv
+
+    def copy(self, piece, block, link):
+        place = self.place
+        view = self.pieces[piece](block)
+        target = (place.up, place.down, place.across, place.sibling)[link]
         return pltpu.make_async_remote_copy(
             src_ref=view,
             dst_ref=view,
-            send_sem=send.at[piece, link, block],
-            recv_sem=recv.at[piece, block],
-            device_id={"expert": links[link][0]},
+            send_sem=self.send.at[piece, link, block],
+            recv_sem=self.recv.at[piece, block],
+            device_id={"expert": target},
             device_id_type=MESH,
         )
 
-    def start(piece, block, which):
-        for link in which:
-            when(links[link][1], lambda link=link: copy(piece, block, link).start())
-
-    def arrive(piece, block):
-        copy(piece, block, SIBLING).wait_recv()
-
-    def mine(z):
-        return place.at(z, place.x, place.core)
-
-    def other(z):
-        return place.at(z, 1 - place.x, place.core)
-
-    def from_across(d):
-        for piece in range(len(pieces)):
-            for z, there in place.by_distance(d):
-
-                def body(z=z, piece=piece):
-                    arrive(piece, other(z))
-                    start(piece, other(z), (SIBLING,))
-
-                when(there, body)
-
-    for piece in range(len(pieces)):
-        start(piece, place.me, (UP, DOWN, ACROSS, SIBLING))
-    for d in range(1, place.height):
-        for piece in range(len(pieces)):
-            for (z, there), onward in zip(place.by_distance(d), (UP, DOWN)):
-
-                def body(z=z, piece=piece, onward=onward):
-                    arrive(piece, mine(z))
-                    start(piece, mine(z), (onward, ACROSS, SIBLING))
-
-                when(there, body)
-        from_across(d - 1)
-    from_across(place.height - 1)
-
-    def finish():
+    def arrive(self, piece, block):
+        self.copy(piece, block, SIBLING).wait_recv()
+
+    def mine(self, z):
+        return self.place.at(z, self.place.x, self.place.core)
+
+    def other(self, z):
+        return self.place.at(z, 1 - self.place.x, self.place.core)
+
+    def begin(self, piece):
+        place, me = self.place, self.place.me
+        pl.when(place.has_up)(lambda: self.copy(piece, me, UP).start())
+        pl.when(place.has_down)(lambda: self.copy(piece, me, DOWN).start())
+        self.copy(piece, me, ACROSS).start()
+        self.copy(piece, me, SIBLING).start()
+
+    def line_step(self, d, piece):
+        place = self.place
+        for (z, there), onward, open_ in zip(
+            place.by_distance(d), (UP, DOWN), (place.has_up, place.has_down)
+        ):
+
+            def body(z=z, onward=onward, open_=open_):
+                self.arrive(piece, self.mine(z))
+                pl.when(open_)(lambda: self.copy(piece, self.mine(z), onward).start())
+                self.copy(piece, self.mine(z), ACROSS).start()
+                self.copy(piece, self.mine(z), SIBLING).start()
+
+            when(there, body)
+
+    def across_step(self, d, piece):
+        for z, there in self.place.by_distance(d):
+
+            def body(z=z):
+                self.arrive(piece, self.other(z))
+                self.copy(piece, self.other(z), SIBLING).start()
+
+            when(there, body)
+
+    def from_sibling(self, z):
+        for piece in range(len(self.pieces)):
+            for x in range(COLUMNS):
+                self.arrive(piece, self.place.at(z, x, 1 - self.place.core))
+
+    def steps(self, piece):
+        height = self.place.height
+        found = []
+        for d in range(1, height):
+            found.append(lambda d=d: self.line_step(d, piece))
+            found.append(lambda d=d: self.across_step(d - 1, piece))
+        found.append(lambda: self.across_step(height - 1, piece))
+        return found
+
+    def settle(self):
+        place = self.place
         for z in range(place.height):
-            for piece in range(len(pieces)):
-                for x in range(COLUMNS):
-                    arrive(piece, place.at(z, x, 1 - place.core))
-                copy(piece, mine(z), ACROSS).wait_send()
-                copy(piece, mine(z), SIBLING).wait_send()
-                copy(piece, other(z), SIBLING).wait_send()
+            for piece in range(len(self.pieces)):
+                self.copy(piece, self.mine(z), ACROSS).wait_send()
+                self.copy(piece, self.mine(z), SIBLING).wait_send()
+                self.copy(piece, self.other(z), SIBLING).wait_send()
                 pl.when(jnp.logical_and(place.has_up, z <= place.z))(
-                    lambda: copy(piece, mine(z), UP).wait_send()
+                    lambda: self.copy(piece, self.mine(z), UP).wait_send()
                 )
                 pl.when(jnp.logical_and(place.has_down, z >= place.z))(
-                    lambda: copy(piece, mine(z), DOWN).wait_send()
+                    lambda: self.copy(piece, self.mine(z), DOWN).wait_send()
                 )
 
-    finish()
+
+def staggered(first, second, lag):
+    for i in range(max(len(first), len(second) + lag)):
+        if i < len(first):
+            first[i]()
+        if i >= lag and i - lag < len(second):
+            second[i - lag]()
 
 
 def scatter(place, part_ref, bufs, sems, leave):
@@ -203,11 +221,9 @@
             device_id_type=MESH,
         ).wait_recv()
 
-    def in_order(body):
-        for d in range(height - 1, -1, -1):
-            for way, (z, there) in enumerate(place.by_distance(d)):
-                for h in range(HALVES):
-                    when(there, lambda z=z, h=h: body(z, h, None if d == 0 else (DOWN, UP)[way]))
+    def planes(d, h, body):
+        for way, (z, there) in enumerate(place.by_distance(d)):
+            when(there, lambda z=z: body(z, h, None if d == 0 else (DOWN, UP)[way]))
 
     def send_core(z, h, way):
         core_copy(z, 1 - place.x, h).start()
@@ -274,11 +290,15 @@
         pl.when(jnp.logical_not(before))(alone)
         line_copy(z, slot, h, target).start()
 
-    in_order(send_core)
-    in_order(send_core_own)
-    in_order(send_across)
-    in_order(send_line)
-    for h in range(HALVES):
+    far_first = list(range(height - 1, -1, -1))
+
+    def begin():
+        for h in range(HALVES):
+            for body in (send_core, send_core_own):
+                for d in far_first:
+                    planes(d, h, body)
+
+    def last(h):
         for step in range(1, dps):
             dp_arrive(lax.rem(dp + step, dps), h)
         total = dp_in[0, spans[h]].astype(f32)
@@ -286,6 +306,16 @@
             total = total + dp_in[index, spans[h]].astype(f32)
         leave(h, spans[h], total)
 
+    def steps(h):
+        found = []
+        for d in far_first:
+            found.append(lambda d=d: planes(d, h, send_across))
+            if d + 1 < height:
+                found.append(lambda d=d: planes(d + 1, h, send_line))
+        found.append(lambda: planes(0, h, send_line))
+        found.append(lambda: last(h))
+        return found
+
     def settle(z, h, way):
         core_copy(z, 0, h).wait_send()
         core_copy(z, 1, h).wait_send()
@@ -293,10 +323,14 @@
         if way is not None:
             line_copy(z, 0, h, place.up).wait_send()
 
-    in_order(settle)
-    for h in range(HALVES):
-        for step in range(1, dps):
-            dp_copy(step, h).wait_send()
+    def finish():
+        for h in range(HALVES):
+            for d in far_first:
+                planes(d, h, settle)
+            for step in range(1, dps):
+                dp_copy(step, h).wait_send()
+
+    return begin, steps, finish
 
 
 def scatter_scratch(n, rows, width):
@@ -319,46 +353,152 @@
     return [lambda block, h=h: ref.at[block, pl.ds(h * rows, rows)] for h in range(HALVES)]
 
 
-def spread_kernel(n, tokens_ref, table_ref, rows_ref, tables_ref, send, recv):
+def forward_kernel(
+    n,
+    capacity,
+    tokens_ref,
+    table_ref,
+    w_gate_ref,
+    w_up_ref,
+    w_down_ref,
+    tables_ref,
+    slot_rows_out,
+    gate_out,
+    up_out,
+    hidden_out,
+    outs_out,
+    rows_ref,
+    slot_rows_ref,
+    gate_ref,
+    up_ref,
+    hidden_ref,
+    outs_ref,
+    send,
+    recv,
+    leaving,
+):
     place = Place(n)
+    group = CORES * COLUMNS
+    bf16, f32 = jnp.bfloat16, jnp.float32
     rows_ref[place.me] = tokens_ref[...]
     tables_ref[place.me] = table_ref[...]
-    greet(place, False)
-    gather(place, [lambda block: tables_ref.at[block]] + token_pieces(rows_ref), send, recv)
+    greet(place)
+    pieces = [lambda block: tables_ref.at[block]] + token_pieces(rows_ref)
+    spread = Gather(place, pieces, send, recv)
+    results = [
+        (slot_rows_ref, slot_rows_out),
+        (gate_ref, gate_out),
+        (up_ref, up_out),
+        (hidden_ref, hidden_out),
+        (outs_ref, outs_out),
+    ]
+
+    def copies_out(z):
+        return [
+            pltpu.make_async_copy(source.at[z], target.at[z], leaving.at[i, z])
+            for i, (source, target) in enumerate(results)
+        ]
+
+    def matches(block):
+        places = tables_ref[block, pl.ds(place.me, 1), :]
+        spots = lax.broadcasted_iota(jnp.int32, (capacity, places.shape[1]), 0).astype(f32)
+        return places == spots
+
+    def compute(z):
+        spread.from_sibling(z)
+        for i in range(group):
+            block = z * group + i
+            select = jnp.where(matches(block), 1.0, 0.0).astype(bf16)
+            slot_rows_ref[z, pl.ds(i * capacity, capacity)] = jnp.dot(
+                select, rows_ref[block], preferred_element_type=f32
+            ).astype(bf16)
+        gate_pre = jnp.dot(slot_rows_ref[z], w_gate_ref[0], preferred_element_type=f32)
+        up_pre = jnp.dot(slot_rows_ref[z], w_up_ref[0], preferred_element_type=f32)
+        gate_ref[z] = gate_pre
+        up_ref[z] = up_pre
+        hidden = (gate_pre * jax.nn.sigmoid(gate_pre) * up_pre).astype(bf16)
+        hidden_ref[z] = hidden
+        part = jnp.dot(hidden, w_down_ref[0], preferred_element_type=f32).astype(bf16)
+        for i in range(group):
+            block = z * group + i
+            gates = tables_ref[block, pl.ds(place.me + n, 1), :]
+            gated = jnp.where(matches(block), gates, 0.0).astype(bf16)
+            outs_ref[z, i] = lax.dot_general(
+                gated,
+                part[i * capacity : (i + 1) * capacity],
+                (((0,), (0,)), ((), ())),
+                preferred_element_type=f32,
+            ).astype(bf16)
+        for copy in copies_out(z):
+            copy.start()
+
+    def compute_at(d):
+        if d == 0:
+            compute(place.z)
+            return
+
+        @pl.loop(0, 2)
+        def _(side):
+            z = place.z + (2 * side - 1) * d
+            pl.when(jnp.logical_and(z >= 0, z < place.height))(lambda: compute(z))
+
+    for piece in range(len(pieces)):
+        spread.begin(piece)
+    for d in range(1, place.height + 1):
+        for piece in range(len(pieces)):
+            if d < place.height:
+                spread.line_step(d, piece)
+            spread.across_step(d - 1, piece)
+        compute_at(d - 1)
+    spread.settle()
+    for z in range(place.height):
+        for copy in copies_out(z):
+            copy.wait()
 
 
 def loss_kernel(n, part_ref, targets_ref, scales_ref, grads_ref, *scratch):
     place = Place(n)
     bufs, sems, (send, recv) = scratch[:6], scratch[6:14], scratch[14:]
-    greet(place, True)
+    greet(place)
+    spread = Gather(place, token_pieces(grads_ref), send, recv)
 
     def leave(h, span, total):
         error = total - targets_ref[span, :].astype(jnp.float32)
         grads_ref[place.me, span] = (scales_ref[span, :] * error).astype(jnp.bfloat16)
-
-    scatter(place, part_ref, bufs, sems, leave)
-    gather(place, token_pieces(grads_ref), send, recv)
+        spread.begin(h)
+
+    begin, steps, finish = scatter(place, part_ref, bufs, sems, leave)
+    begin()
+    staggered(steps(0) + spread.steps(0), steps(1) + spread.steps(1), LAG)
+    for z in range(place.height):
+        spread.from_sibling(z)
+    spread.settle()
+    finish()
 
 
 def return_kernel(n, part_ref, out_ref, *scratch):
     place = Place(n)
     bufs, sems = scratch[:6], scratch[6:14]
-    greet(place, True)
+    greet(place)
 
     def leave(h, span, total):
         out_ref[span, :] = total.astype(jnp.bfloat16)
 
-    scatter(place, part_ref, bufs, sems, leave)
+    begin, steps, finish = scatter(place, part_ref, bufs, sems, leave)
+    begin()
+    staggered(steps(0), steps(1), 1)
+    finish()
 
 
 def run(kernel, out_shape, scratch, number, *operands):
     single = not isinstance(out_shape, (list, tuple))
     whole = pl.BlockSpec(memory_space=pltpu.VMEM)
+    outside = pl.BlockSpec(memory_space=pl.ANY)
     return pl.pallas_call(
         kernel,
         out_shape=out_shape,
         in_specs=[whole] * len(operands),
-        out_specs=whole if single else [whole] * len(out_shape),
+        out_specs=whole if single else [whole] + [outside] * (len(out_shape) - 1),
         scratch_shapes=scratch,
         compiler_params=pltpu.CompilerParams(
             collective_id=number, has_side_effects=True, vmem_limit_bytes=60 * 2**20
@@ -376,7 +516,7 @@
     )
     places = jnp.where(chosen, places, -1.0)
     gates = jnp.sum(jnp.where(hits, route_gates.astype(jnp.float32)[None], 0.0), 2)
-    return jnp.concatenate([places, gates], 0).astype(jnp.bfloat16)
+    return jnp.concatenate([places, gates], 0)
 
 
 def block_dot(left, right, contract):
@@ -394,27 +534,42 @@
     contract_first = (((0,), (0,)), ((), ()))
 
     table = table_of(routes, route_gates, n)
-    rows, tables = run(
-        functools.partial(spread_kernel, n),
-        [jax.ShapeDtypeStruct((n, count, width), bf16), jax.ShapeDtypeStruct((n, 2 * n, count), bf16)],
-        gather_scratch(n, HALVES + 1),
+    height = n // (CORES * COLUMNS)
+    slots = n * capacity // height
+    hidden_width = w_gate.shape[2]
+    shapes = [
+        ((height, slots, width), bf16),
+        ((height, slots, hidden_width), f32),
+        ((height, slots, hidden_width), f32),
+        ((height, slots, hidden_width), bf16),
+        ((height, n // height, count, width), bf16),
+    ]
+    tables, slot_rows, gate_pre, up_pre, hidden, outs = run(
+        functools.partial(forward_kernel, n, capacity),
+        [jax.ShapeDtypeStruct((n, 2 * n, count), f32)]
+        + [jax.ShapeDtypeStruct(*shape) for shape in shapes],
+        [pltpu.VMEM((n, count, width), bf16)]
+        + [pltpu.VMEM(*shape) for shape in shapes]
+        + gather_scratch(n, HALVES + 1)
+        + [pltpu.SemaphoreType.DMA((len(shapes), height))],
         0,
         tokens,
         table,
+        w_gate,
+        w_up,
+        w_down,
     )
+    slot_rows = slot_rows.reshape(n * capacity, width)
+    gate_pre, up_pre, hidden = (
+        item.reshape(n * capacity, hidden_width) for item in (gate_pre, up_pre, hidden)
+    )
+    outs = outs.reshape(n, count, width)
     me = lax.axis_index("expert")
     places = lax.dynamic_index_in_dim(tables, me, 1, keepdims=True)
     gates = lax.dynamic_index_in_dim(tables, me + n, 1, keepdims=True)
-    matches = places.astype(jnp.int32) == jnp.arange(capacity, dtype=jnp.int32)[None, :, None]
+    matches = places == jnp.arange(capacity, dtype=f32)[None, :, None]
     select = matches.astype(bf16)
-    gated = jnp.where(matches, gates, jnp.zeros((), bf16))
-
-    slot_rows = block_dot(select, rows, ((2,), (1,))).reshape(n * capacity, width)
-    gate_pre = jnp.dot(slot_rows, w_gate[0], preferred_element_type=f32)
-    up_pre = jnp.dot(slot_rows, w_up[0], preferred_element_type=f32)
-    hidden = (jax.nn.silu(gate_pre) * up_pre).astype(bf16)
-    part = jnp.dot(hidden, w_down[0], preferred_element_type=f32).astype(bf16)
-    outs = block_dot(gated, part.reshape(n, capacity, width), ((1,), (1,)))
+    gated = jnp.where(matches, gates, 0.0).astype(bf16)
 
     picks = domains[:, None] == jnp.arange(domain_weight.shape[0], dtype=jnp.int32)[None, :]
     scales = jnp.sum(jnp.where(picks, domain_weight[None, :], 0.0), 1, keepdims=True)

time: 171 us -> 169 us (0.988)
  matrix products: 30.2 us -> 18.7 us
  Pallas kernels: 133 us -> 141 us
    pallas_call x3, Pallas kernels: 133 us -> 141 us  [run(): pl.pallas_call(kernel, out_shape=out_shape, in_specs=[whole] * len(operan...]
    dot_general x4 -> x2, matrix products: 12.5 us -> 6.28 us  [block_dot(): lax.dot_general(left, right, ((contract[0], contract[1]), ((0,), (0,))),...]
    dot_general x3 -> x0, matrix products: 5.27 us -> none  [the longest x1 2.76 us: shards(): up_pre = jnp.dot(slot_rows, w_up[0], preferred_element_type=f32)]
where the time goes in v3:
time: 169 us; the launch traced here: 168 us
  Pallas kernels  141 us (83%)
  matrix products  18.7 us (11%)
  local copies, waits for them, and re-layouts  4.06 us (2%)
  other arithmetic  3.46 us (2%)
    pallas_call x3, Pallas kernels, run(): pl.pallas_call(kernel, out_shape=out_shape, in_specs=[whole] * len(operan...  141 us
    dot_general x2, matrix products, block_dot(): lax.dot_general(left, right, ((contract[0], contract[1]), ((0,), (0,))),...  6.28 us

profile of v3, /device:TPU:0, one launch (start us, length us, event | category | flops | bytes accessed | tf_op | source)
XLA Modules:
  0.0 168.3 jit_solution(8607432684227666360)
XLA Ops:
  0.6 0.8 select_reduce_fusion.1
  1.4 0.7 fusion.18
  2.1 0.7 convert_element_type.24
  2.8 0.7 select_reduce_fusion
  3.5 0.1 convolution_select_fusion
  3.6 0.6 pad_maximum_fusion.table_ref
  4.2 0.7 copy.16.scales_ref
  5.0 37.5 %shard_map.120 = (f32[16,32,128]{2,1,0:T(8,128)}, bf16[4,256,1024]{2,1,0:T(8,128)(2,1)}, f32[4,256,512]{2,1,0:T(8,128)}, f32[4,256,512]{2,1,0:T(8,128)}, bf16[4,...) custom-call(bf16[128,1024]{1,0:T(8,128)(2,1)} %tokens_ref.1, f32[32,128]{1,0:T(8,128)} %pad_maximum_fusion.table_ref, ...), custom_call_target="tpu_custom_call" | custom-call | tf_op jit(solution)/shard_map/pallas_call | solution.py:497
  42.5 0.9 constant_dynamic-slice_fusion.1
  43.4 66.8 %shard_map.121 = bf16[16,128,1024]{2,1,0:T(8,128)(2,1)} custom-call(bf16[16,128,1024]{2,1,0:T(8,128)(2,1)} %bitcast.70, bf16[128,1024]{1,0:T(8,128)(2,1)} %targets_ref.1, f32[128,1]{1,0:T(8,128)} %copy.16.scales_ref), custom_call_target="tpu_custom_call" | custom-call | tf_op jit(solution)/shard_map/pallas_call | solution.py:497
  110.1 0.0 copy-start.2
  110.2 0.0 copy-start.5
  110.2 3.0 %convolution_convert_fusion.1 = bf16[16,64,1024]{2,1,0:T(8,128)(2,1)S(1)} fusion(bf16[16,128,1024]{2,1,0:T(8,128)(2,1)} %shard_map.121, f32[16,128]{1,0:T(8,128)S(1)} %bitcast.74, f32[16,128]{1,0:T(8,128)S(1)} %bitcast.72), kind=kOutput, calls=%fused_computation.15 | convolution fusion | flops 269746176 | bytes 6307840 | tf_op jit(solution)/shard_map/dot_general | solution.py:523
  113.2 0.1 copy-done.5
  113.3 0.6 copy-done.6
  114.0 1.9 %fusion.7 = (bf16[1024,512]{1,0:T(8,128)(2,1)S(1)}, bf16[1024,512]{1,0:T(8,128)(2,1)S(1)}) fusion(f32[4,256,512]{2,1,0:T(8,128)S(1)} %copy-done.5, f32[4,256,512]{2,1,0:T(8,128)S(1)} %copy-done.6, bf16[1024,1024]{1,0:T(8,128)(2,1)S(1)} %bitcast.67, bf16[1,512,1024]{2,1,0:T(8,128)(2,1)S(1)} %copy-done.2), kind=kOutput, calls=%fused_computation.12 | convolution fusion | flops 1080557568 | bytes 9437184 | tf_op jit(solution)/shard_map/dot_general | solution.py:588
  115.9 2.6 %convolution_bitcast_fusion = f32[1,512,1024]{2,1,0:T(8,128)} fusion(bf16[1024,512]{1,0:T(8,128)(2,1)S(1)} %bitcast.71, bf16[1024,1024]{1,0:T(8,128)(2,1)S(1)} %bitcast.68), kind=kOutput, calls=%fused_computation.16 | convolution fusion | flops 1073741824 | bytes 5242880 | tf_op jit(solution)/shard_map/dot_general | solution.py:602
  118.5 2.6 %convolution_bitcast_fusion.1 = f32[1,1024,512]{2,1,0:T(8,128)} fusion(bf16[1024,1024]{1,0:T(8,128)(2,1)S(1)} %bitcast.76, bf16[1024,512]{1,0:T(8,128)(2,1)S(1)} %get-tuple-element.16), kind=kOutput, calls=%fused_computation.17 | convolution fusion | flops 1073741824 | bytes 5242880 | tf_op jit(solution)/shard_map/dot_general | solution.py:604
  121.1 2.6 %convolution_bitcast_fusion.2 = f32[1,1024,512]{2,1,0:T(8,128)} fusion(bf16[1024,1024]{1,0:T(8,128)(2,1)S(1)} %bitcast.77, bf16[1024,512]{1,0:T(8,128)(2,1)S(1)} %get-tuple-element.17), kind=kOutput, calls=%fused_computation.18 | convolution fusion | flops 1073741824 | bytes 5242880 | tf_op jit(solution)/shard_map/dot_general | solution.py:603
  123.8 1.3 fusion.10
  125.1 1.3 add_convert_fusion
  126.3 3.2 %convolution_convert_fusion.part_ref = bf16[16,128,1024]{2,1,0:T(8,128)(2,1)} fusion(bf16[16,64,1024]{2,1,0:T(8,128)(2,1)S(1)} %bitcast.69, f32[16,128]{1,0:T(8,128)S(1)} %bitcast.73), kind=kOutput, calls=%fused_computation.1 | convolution fusion | flops 270663680 | bytes 6299648 | tf_op jit(solution)/shard_map/dot_general | solution.py:523
  129.6 37.1 %shard_map.122 = bf16[128,1024]{1,0:T(8,128)(2,1)} custom-call(bf16[16,128,1024]{2,1,0:T(8,128)(2,1)} %convolution_convert_fusion.part_ref), custom_call_target="tpu_custom_call" | custom-call | tf_op jit(solution)/shard_map/pallas_call | solution.py:497
  166.6 1.7 copy.18
  (10 shorter events, 0.0 us)
Async XLA Ops:
  110.1 3.1 %copy-start.2 = (bf16[1,512,1024]{2,1,0:T(8,128)(2,1)S(1)}, bf16[1,512,1024]{2,1,0:T(8,128)(2,1)}, u32[]{:S(2)}) copy-start(bf16[1,512,1024]{2,1,0:T(8,128)(2,1)} %w_down_ref.1) | copy-start | bytes 3145732
  110.2 3.2 %copy-start.5 = (f32[4,256,512]{2,1,0:T(8,128)S(1)}, f32[4,256,512]{2,1,0:T(8,128)}, u32[]{:S(2)}) copy-start(f32[4,256,512]{2,1,0:T(8,128)} %get-tuple-element.13) | copy-start | bytes 6291460
  110.2 3.8 %copy-start.6 = (f32[4,256,512]{2,1,0:T(8,128)S(1)}, f32[4,256,512]{2,1,0:T(8,128)}, u32[]{:S(2)}) copy-start(f32[4,256,512]{2,1,0:T(8,128)} %get-tuple-element.12) | copy-start | bytes 6291460
  114.0 1.9 %copy-start.1 = (bf16[4,256,512]{2,1,0:T(8,128)(2,1)S(1)}, bf16[4,256,512]{2,1,0:T(8,128)(2,1)}, u32[]{:S(2)}) copy-start(bf16[4,256,512]{2,1,0:T(8,128)(2,1)} %get-tuple-element.15) | copy-start | bytes 3145732
  115.9 2.6 %copy-start.4 = (bf16[4,256,1024]{2,1,0:T(8,128)(2,1)S(1)}, bf16[4,256,1024]{2,1,0:T(8,128)(2,1)}, u32[]{:S(2)}) copy-start(bf16[4,256,1024]{2,1,0:T(8,128)(2,1)} %get-tuple-element.14) | copy-start | bytes 6291460
  121.1 2.6 %copy-start.3 = (bf16[1,1024,512]{2,1,0:T(8,128)(2,1)S(1)}, bf16[1,1024,512]{2,1,0:T(8,128)(2,1)}, u32[]{:S(2)}) copy-start(bf16[1,1024,512]{2,1,0:T(8,128)(2,1)} %w_gate_ref.1) | copy-start | bytes 3145732
  123.8 1.3 copy-start

commit v4 on v3

--- a/solution.py
+++ b/solution.py
@@ -1,4 +1,5 @@
 import functools
+import math
 
 import jax
 import jax.numpy as jnp
@@ -11,7 +12,6 @@
 CORES = 2
 COLUMNS = 2
 HALVES = 2
-LAG = 4
 UP, DOWN, ACROSS, SIBLING = range(4)
 
 
@@ -134,6 +134,26 @@
         found.append(lambda: self.across_step(height - 1, piece))
         return found
 
+    def run(self, compute, loads):
+        place = self.place
+        for d in range(1, place.height + 1):
+            for piece in range(len(self.pieces)):
+                if d < place.height:
+                    self.line_step(d, piece)
+                self.across_step(d - 1, piece)
+            if d == 1:
+                for copy in loads:
+                    copy.wait()
+                compute(place.z)
+                continue
+
+            @pl.loop(0, 2)
+            def _(side, d=d):
+                z = place.z + (2 * side - 1) * (d - 1)
+                pl.when(jnp.logical_and(z >= 0, z < place.height))(lambda: compute(z))
+
+        self.settle()
+
     def settle(self):
         place = self.place
         for z in range(place.height):
@@ -353,14 +373,31 @@
     return [lambda block, h=h: ref.at[block, pl.ds(h * rows, rows)] for h in range(HALVES)]
 
 
+def load(sems, *pairs):
+    copies = [
+        pltpu.make_async_copy(source, target, sems.at[i])
+        for i, (source, target) in enumerate(pairs)
+    ]
+    for copy in copies:
+        copy.start()
+    return copies
+
+
+def table_matches(place, tables_ref, block, capacity):
+    places = tables_ref[block, pl.ds(place.me, 1), :]
+    spots = lax.broadcasted_iota(jnp.int32, (capacity, places.shape[1]), 0).astype(jnp.float32)
+    return places == spots
+
+
 def forward_kernel(
     n,
     capacity,
     tokens_ref,
-    table_ref,
-    w_gate_ref,
-    w_up_ref,
-    w_down_ref,
+    routes_ref,
+    gates_ref,
+    w_gate_in,
+    w_up_in,
+    w_down_in,
     tables_ref,
     slot_rows_out,
     gate_out,
@@ -373,15 +410,22 @@
     up_ref,
     hidden_ref,
     outs_ref,
+    w_gate_ref,
+    w_up_ref,
+    w_down_ref,
     send,
     recv,
     leaving,
+    loading,
 ):
     place = Place(n)
     group = CORES * COLUMNS
     bf16, f32 = jnp.bfloat16, jnp.float32
+    loads = load(
+        loading, (w_gate_in, w_gate_ref), (w_up_in, w_up_ref), (w_down_in, w_down_ref)
+    )
     rows_ref[place.me] = tokens_ref[...]
-    tables_ref[place.me] = table_ref[...]
+    tables_ref[place.me] = table_of(routes_ref[...], gates_ref[...].astype(f32), n)
     greet(place)
     pieces = [lambda block: tables_ref.at[block]] + token_pieces(rows_ref)
     spread = Gather(place, pieces, send, recv)
@@ -400,9 +444,7 @@
         ]
 
     def matches(block):
-        places = tables_ref[block, pl.ds(place.me, 1), :]
-        spots = lax.broadcasted_iota(jnp.int32, (capacity, places.shape[1]), 0).astype(f32)
-        return places == spots
+        return table_matches(place, tables_ref, block, capacity)
 
     def compute(z):
         spread.from_sibling(z)
@@ -432,25 +474,122 @@
         for copy in copies_out(z):
             copy.start()
 
-    def compute_at(d):
-        if d == 0:
-            compute(place.z)
-            return
-
-        @pl.loop(0, 2)
-        def _(side):
-            z = place.z + (2 * side - 1) * d
-            pl.when(jnp.logical_and(z >= 0, z < place.height))(lambda: compute(z))
-
     for piece in range(len(pieces)):
         spread.begin(piece)
-    for d in range(1, place.height + 1):
-        for piece in range(len(pieces)):
-            if d < place.height:
-                spread.line_step(d, piece)
-            spread.across_step(d - 1, piece)
-        compute_at(d - 1)
-    spread.settle()
+    spread.run(compute, loads)
+    for z in range(place.height):
+        for copy in copies_out(z):
+            copy.wait()
+
+
+def middle_kernel(
+    n,
+    capacity,
+    targets_ref,
+    scales_ref,
+    tables_ref,
+    part_in,
+    gate_in,
+    up_in,
+    w_gate_in,
+    w_up_in,
+    w_down_in,
+    slot_grads_out,
+    gate_grad_out,
+    up_grad_out,
+    backs_out,
+    grads_ref,
+    part_ref,
+    gate_ref,
+    up_ref,
+    w_gate_ref,
+    w_up_ref,
+    w_down_ref,
+    slot_grads_ref,
+    gate_grad_ref,
+    up_grad_ref,
+    *scratch,
+):
+    place = Place(n)
+    group = CORES * COLUMNS
+    bf16, f32 = jnp.bfloat16, jnp.float32
+    contract_last = (((1,), (1,)), ((), ()))
+    bufs, sems, (send, recv, leaving, loading) = scratch[:6], scratch[6:14], scratch[14:]
+    loads = load(
+        loading,
+        (part_in, part_ref),
+        (gate_in, gate_ref),
+        (up_in, up_ref),
+        (w_gate_in, w_gate_ref),
+        (w_up_in, w_up_ref),
+        (w_down_in, w_down_ref),
+    )
+    greet(place)
+    spread = Gather(place, token_pieces(grads_ref), send, recv)
+    loads[0].wait()
+
+    def leave(h, span, total):
+        error = total - targets_ref[span, :].astype(f32)
+        grads_ref[place.me, span] = (scales_ref[span, :] * error).astype(bf16)
+        spread.begin(h)
+
+    begin, steps, finish = scatter(place, part_ref, bufs, sems, leave)
+    begin()
+    staggered(steps(0), steps(1), 1)
+    finish()
+
+    def copies_out(z):
+        blocks = pl.ds(z * group, group)
+        pairs = [
+            (slot_grads_ref.at[z], slot_grads_out.at[z]),
+            (gate_grad_ref.at[z], gate_grad_out.at[z]),
+            (up_grad_ref.at[z], up_grad_out.at[z]),
+            (part_ref.at[blocks], backs_out.at[blocks]),
+        ]
+        return [
+            pltpu.make_async_copy(source, target, leaving.at[i, z])
+            for i, (source, target) in enumerate(pairs)
+        ]
+
+    def compute(z):
+        spread.from_sibling(z)
+        for i in range(group):
+            block = z * group + i
+            gates = tables_ref[block, pl.ds(place.me + n, 1), :]
+            hits = table_matches(place, tables_ref, block, capacity)
+            slot_grads_ref[z, pl.ds(i * capacity, capacity)] = jnp.dot(
+                jnp.where(hits, gates, 0.0).astype(bf16), grads_ref[block], preferred_element_type=f32
+            ).astype(bf16)
+        hidden_grad = lax.dot_general(
+            slot_grads_ref[z], w_down_ref[0], contract_last, preferred_element_type=f32
+        )
+        gate_pre = gate_ref[z]
+        sigma = jax.nn.sigmoid(gate_pre)
+        gate_grad = hidden_grad * up_ref[z] * sigma * (1.0 + gate_pre * (1.0 - sigma))
+        gate_grad = gate_grad.astype(bf16)
+        up_grad = (hidden_grad * gate_pre * sigma).astype(bf16)
+        gate_grad_ref[z] = gate_grad
+        up_grad_ref[z] = up_grad
+        row_part = lax.dot_general(
+            gate_grad, w_gate_ref[0], contract_last, preferred_element_type=f32
+        )
+        row_part = row_part + lax.dot_general(
+            up_grad, w_up_ref[0], contract_last, preferred_element_type=f32
+        )
+        row_part = row_part.astype(bf16)
+        for i in range(group):
+            block = z * group + i
+            hits = table_matches(place, tables_ref, block, capacity)
+            part_ref[block] = lax.dot_general(
+                jnp.where(hits, 1.0, 0.0).astype(bf16),
+                row_part[i * capacity : (i + 1) * capacity],
+                (((0,), (0,)), ((), ())),
+                preferred_element_type=f32,
+            ).astype(bf16)
+        for copy in copies_out(z):
+            copy.start()
+
+    spread.run(compute, loads[1:])
     for z in range(place.height):
         for copy in copies_out(z):
             copy.wait()
@@ -469,7 +608,7 @@
 
     begin, steps, finish = scatter(place, part_ref, bufs, sems, leave)
     begin()
-    staggered(steps(0) + spread.steps(0), steps(1) + spread.steps(1), LAG)
+    staggered(steps(0) + spread.steps(0), steps(1) + spread.steps(1), 4)
     for z in range(place.height):
         spread.from_sibling(z)
     spread.settle()
@@ -490,15 +629,19 @@
     finish()
 
 
-def run(kernel, out_shape, scratch, number, *operands):
-    single = not isinstance(out_shape, (list, tuple))
+def run(kernel, out_shape, scratch, number, *operands, in_vmem=None, out_vmem=None):
     whole = pl.BlockSpec(memory_space=pltpu.VMEM)
     outside = pl.BlockSpec(memory_space=pl.ANY)
+
+    def places(count, near):
+        near = count if near is None else near
+        return [whole] * near + [outside] * (count - near)
+
     return pl.pallas_call(
         kernel,
         out_shape=out_shape,
-        in_specs=[whole] * len(operands),
-        out_specs=whole if single else [whole] + [outside] * (len(out_shape) - 1),
+        in_specs=places(len(operands), in_vmem),
+        out_specs=places(len(out_shape), out_vmem),
         scratch_shapes=scratch,
         compiler_params=pltpu.CompilerParams(
             collective_id=number, has_side_effects=True, vmem_limit_bytes=60 * 2**20
@@ -506,17 +649,23 @@
     )(*operands)
 
 
-def table_of(routes, route_gates, experts):
-    count = routes.shape[0]
-    hits = routes[None, :, :] == jnp.arange(experts, dtype=jnp.int32)[:, None, None]
-    chosen = jnp.any(hits, 2)
-    earlier = jnp.arange(count)[:, None] < jnp.arange(count)[None, :]
+def table_of(routes, gates, experts):
+    top, count = routes.shape
+    ids = lax.broadcasted_iota(jnp.int32, (experts, count), 0)
+    chosen = jnp.zeros((experts, count), jnp.float32)
+    weights = jnp.zeros((experts, count), jnp.float32)
+    for k in range(top):
+        hit = routes[k : k + 1, :] == ids
+        chosen = jnp.where(hit, 1.0, chosen)
+        weights = jnp.where(hit, gates[k : k + 1, :], weights)
+    square = (count, count)
+    earlier = lax.broadcasted_iota(jnp.int32, square, 0) < lax.broadcasted_iota(jnp.int32, square, 1)
     places = jnp.dot(
-        chosen.astype(jnp.bfloat16), earlier.astype(jnp.bfloat16), preferred_element_type=jnp.float32
+        chosen.astype(jnp.bfloat16),
+        jnp.where(earlier, 1.0, 0.0).astype(jnp.bfloat16),
+        preferred_element_type=jnp.float32,
     )
-    places = jnp.where(chosen, places, -1.0)
-    gates = jnp.sum(jnp.where(hits, route_gates.astype(jnp.float32)[None], 0.0), 2)
-    return jnp.concatenate([places, gates], 0)
+    return jnp.concatenate([jnp.where(chosen > 0.0, places, -1.0), weights], 0)
 
 
 def block_dot(left, right, contract):
@@ -530,10 +679,10 @@
     n = lax.axis_size("expert")
     capacity = max(2, 4 * count * routes.shape[1] // (3 * n))
     bf16, f32 = jnp.bfloat16, jnp.float32
+    weights = (w_gate, w_up, w_down)
     contract_last = (((1,), (1,)), ((), ()))
     contract_first = (((0,), (0,)), ((), ()))
 
-    table = table_of(routes, route_gates, n)
     height = n // (CORES * COLUMNS)
     slots = n * capacity // height
     hidden_width = w_gate.shape[2]
@@ -550,51 +699,90 @@
         + [jax.ShapeDtypeStruct(*shape) for shape in shapes],
         [pltpu.VMEM((n, count, width), bf16)]
         + [pltpu.VMEM(*shape) for shape in shapes]
+        + [pltpu.VMEM(item.shape, bf16) for item in weights]
         + gather_scratch(n, HALVES + 1)
-        + [pltpu.SemaphoreType.DMA((len(shapes), height))],
+        + [pltpu.SemaphoreType.DMA((len(shapes), height)), pltpu.SemaphoreType.DMA((3,))],
         0,
         tokens,
-        table,
-        w_gate,
-        w_up,
-        w_down,
+        routes.T,
+        route_gates.T,
+        *weights,
+        in_vmem=3,
+        out_vmem=1,
     )
+    outs = outs.reshape(n, count, width)
+    picks = domains[:, None] == jnp.arange(domain_weight.shape[0], dtype=jnp.int32)[None, :]
+    scales = jnp.sum(jnp.where(picks, domain_weight[None, :], 0.0), 1, keepdims=True)
+    bufs, sems = scatter_scratch(n, count, width)
+    grad_shapes = [
+        ((height, slots, width), bf16),
+        ((height, slots, hidden_width), bf16),
+        ((height, slots, hidden_width), bf16),
+    ]
+    needed = (
+        [((n, count, width), bf16)] * 2
+        + [((height, slots, hidden_width), f32)] * 2
+        + [(item.shape, bf16) for item in weights]
+        + grad_shapes
+    )
+    fits = sum(math.prod(shape) * (4 if kind == f32 else 2) for shape, kind in needed)
+    fits = fits + sum(math.prod(buf.shape) * 2 for buf in bufs) < 48 * 2**20
+    if fits:
+        slot_grads, gate_grad, up_grad, backs = run(
+            functools.partial(middle_kernel, n, capacity),
+            [jax.ShapeDtypeStruct(*shape) for shape in grad_shapes + needed[:1]],
+            [pltpu.VMEM(*shape) for shape in needed]
+            + bufs
+            + sems
+            + gather_scratch(n, HALVES)
+            + [pltpu.SemaphoreType.DMA((4, height)), pltpu.SemaphoreType.DMA((6,))],
+            1,
+            targets,
+            scales,
+            tables,
+            outs,
+            gate_pre,
+            up_pre,
+            *weights,
+            in_vmem=3,
+            out_vmem=0,
+        )
+        slot_grads = slot_grads.reshape(n * capacity, width)
+        gate_grad = gate_grad.reshape(n * capacity, hidden_width)
+        up_grad = up_grad.reshape(n * capacity, hidden_width)
     slot_rows = slot_rows.reshape(n * capacity, width)
     gate_pre, up_pre, hidden = (
         item.reshape(n * capacity, hidden_width) for item in (gate_pre, up_pre, hidden)
     )
-    outs = outs.reshape(n, count, width)
-    me = lax.axis_index("expert")
-    places = lax.dynamic_index_in_dim(tables, me, 1, keepdims=True)
-    gates = lax.dynamic_index_in_dim(tables, me + n, 1, keepdims=True)
-    matches = places == jnp.arange(capacity, dtype=f32)[None, :, None]
-    select = matches.astype(bf16)
-    gated = jnp.where(matches, gates, 0.0).astype(bf16)
-
-    picks = domains[:, None] == jnp.arange(domain_weight.shape[0], dtype=jnp.int32)[None, :]
-    scales = jnp.sum(jnp.where(picks, domain_weight[None, :], 0.0), 1, keepdims=True)
-    bufs, sems = scatter_scratch(n, count, width)
-    loss_grads = run(
-        functools.partial(loss_kernel, n),
-        jax.ShapeDtypeStruct((n, count, width), bf16),
-        bufs + sems + gather_scratch(n, HALVES),
-        1,
-        outs,
-        targets,
-        scales,
-    )
-
-    slot_grads = block_dot(gated, loss_grads, ((2,), (1,))).reshape(n * capacity, width)
-    hidden_grad = lax.dot_general(slot_grads, w_down[0], contract_last, preferred_element_type=f32)
-    sigma = jax.nn.sigmoid(gate_pre)
-    gate_grad = (hidden_grad * up_pre * sigma * (1.0 + gate_pre * (1.0 - sigma))).astype(bf16)
-    up_grad = (hidden_grad * gate_pre * sigma).astype(bf16)
-    row_part = lax.dot_general(gate_grad, w_gate[0], contract_last, preferred_element_type=f32)
-    row_part = row_part + lax.dot_general(up_grad, w_up[0], contract_last, preferred_element_type=f32)
-    backs = block_dot(select, row_part.astype(bf16).reshape(n, capacity, width), ((1,), (1,)))
-    grad_tokens = run(
+    if not fits:
+        me = lax.axis_index("expert")
+        places = lax.dynamic_index_in_dim(tables, me, 1, keepdims=True)
+        gates = lax.dynamic_index_in_dim(tables, me + n, 1, keepdims=True)
+        matches = places == jnp.arange(capacity, dtype=f32)[None, :, None]
+        select = matches.astype(bf16)
+        gated = jnp.where(matches, gates, 0.0).astype(bf16)
+
+        (loss_grads,) = run(
+            functools.partial(loss_kernel, n),
+            [jax.ShapeDtypeStruct((n, count, width), bf16)],
+            bufs + sems + gather_scratch(n, HALVES),
+            1,
+            outs,
+            targets,
+            scales,
+        )
+
+        slot_grads = block_dot(gated, loss_grads, ((2,), (1,))).reshape(n * capacity, width)
+        hidden_grad = lax.dot_general(slot_grads, w_down[0], contract_last, preferred_element_type=f32)
+        sigma = jax.nn.sigmoid(gate_pre)
+        gate_grad = (hidden_grad * up_pre * sigma * (1.0 + gate_pre * (1.0 - sigma))).astype(bf16)
+        up_grad = (hidden_grad * gate_pre * sigma).astype(bf16)
+        row_part = lax.dot_general(gate_grad, w_gate[0], contract_last, preferred_element_type=f32)
+        row_part = row_part + lax.dot_general(up_grad, w_up[0], contract_last, preferred_element_type=f32)
+        backs = block_dot(select, row_part.astype(bf16).reshape(n, capacity, width), ((1,), (1,)))
+    (grad_tokens,) = run(
         functools.partial(return_kernel, n),
-        jax.ShapeDtypeStruct((count, width), bf16),
+        [jax.ShapeDtypeStruct((count, width), bf16)],
         bufs + sems,
         2,
         backs,

time: 169 us -> 151 us (0.89)
  matrix products: 18.7 us -> 7.79 us
  other arithmetic: 3.46 us -> 0.76 us
  local copies, waits for them, and re-layouts: 4.06 us -> 1.47 us
    dot_general x6 -> x0, matrix products: 10.9 us -> none  [the longest x2 6.28 us: block_dot(): lax.dot_general(left, right, ((contract[0], contract[1]), ((0,), (0,))),...]
    unnamed x15 -> x13, local copies, waits for them, and re-layouts: 2.42 us -> 0.73 us
where the time goes in v4:
time: 151 us
  Pallas kernels  140 us (93%)
  matrix products  7.79 us (5%)
    pallas_call x3, Pallas kernels, run(): pl.pallas_call(kernel, out_shape=out_shape, in_specs=places(len(operands)...  140 us

profile of v4, /device:TPU:0, one launch (start us, length us, event | category | flops | bytes accessed | tf_op | source)
XLA Modules:
  0.0 151.2 jit_solution(6939948048938951321)
XLA Ops:
  0.6 0.8 select_reduce_fusion
  1.4 0.7 copy.17.scales_ref
  2.1 36.6 %shard_map.120 = (f32[16,32,128]{2,1,0:T(8,128)}, bf16[4,256,1024]{2,1,0:T(8,128)(2,1)}, f32[4,256,512]{2,1,0:T(8,128)}, f32[4,256,512]{2,1,0:T(8,128)}, bf16[4,...) custom-call(bf16[128,1024]{1,0:T(8,128)(2,1)} %tokens_ref.1, s32[6,128]{1,0:T(8,128)} %bitcast.20, ...), custom_call_target="tpu_custom_call" | custom-call | tf_op jit(solution)/shard_map/pallas_call | solution.py:640
  38.7 64.8 %shard_map.121 = (bf16[4,256,1024]{2,1,0:T(8,128)(2,1)}, bf16[4,256,512]{2,1,0:T(8,128)(2,1)}, bf16[4,256,512]{2,1,0:T(8,128)(2,1)}, bf16[16,128,1024]{2,1,0:T(8,128)(2,1)}) custom-call(bf16[128,1024]{1,0:T(8,128)(2,1)} %targets_ref.1, f32[128,1]{1,0:T(8,128)} %copy.17.scales_ref, f32[16,32,128]{2,1,0:T(8,128)} %get-tuple-element.14.tables_ref, ...), custom_call_target="tpu_custom_call" | custom-call | tf_op jit(solution)/shard_map/pallas_call | solution.py:640
  103.5 0.0 copy-start
  103.5 0.0 copy-start.1
  103.5 39.1 %shard_map.122 = bf16[128,1024]{1,0:T(8,128)(2,1)} custom-call(bf16[16,128,1024]{2,1,0:T(8,128)(2,1)} %get-tuple-element.18.part_ref), custom_call_target="tpu_custom_call" | custom-call | tf_op jit(solution)/shard_map/pallas_call | solution.py:640
  142.6 0.0 copy-done
  142.6 0.0 copy-done.1
  142.6 0.0 copy-start.3
  142.6 0.0 copy-start.5
  142.6 2.6 %convolution_bitcast_fusion = f32[1,512,1024]{2,1,0:T(8,128)} fusion(bf16[4,256,512]{2,1,0:T(8,128)(2,1)S(1)} %copy-done.1, bf16[4,256,1024]{2,1,0:T(8,128)(2,1)S(1)} %copy-done), kind=kOutput, calls=%fused_computation | convolution fusion | flops 1073741824 | bytes 5242880 | tf_op jit(solution)/shard_map/dot_general | solution.py:790
  145.2 0.0 copy-done.3
  145.2 0.0 copy-done.5
  145.2 0.0 copy-start.4
  145.2 2.6 %convolution_bitcast_fusion.2 = f32[1,1024,512]{2,1,0:T(8,128)} fusion(bf16[4,256,1024]{2,1,0:T(8,128)(2,1)S(1)} %copy-done.3, bf16[4,256,512]{2,1,0:T(8,128)(2,1)S(1)} %copy-done.5), kind=kOutput, calls=%fused_computation.2 | convolution fusion | flops 1073741824 | bytes 5242880 | tf_op jit(solution)/shard_map/dot_general | solution.py:791
  147.8 0.0 copy-done.4
  147.8 0.0 copy-start.2
  147.8 2.6 %convolution_bitcast_fusion.1 = f32[1,1024,512]{2,1,0:T(8,128)} fusion(bf16[4,256,1024]{2,1,0:T(8,128)(2,1)S(1)} %copy-done.3, bf16[4,256,512]{2,1,0:T(8,128)(2,1)S(1)} %copy-done.4), kind=kOutput, calls=%fused_computation.1 | convolution fusion | flops 1073741824 | bytes 5242880 | tf_op jit(solution)/shard_map/dot_general | solution.py:792
  150.4 0.0 copy-done.2
  150.5 0.7 copy.25
Async XLA Ops:
  103.5 39.1 %copy-start = (bf16[4,256,1024]{2,1,0:T(8,128)(2,1)S(1)}, bf16[4,256,1024]{2,1,0:T(8,128)(2,1)}, u32[]{:S(2)}) copy-start(bf16[4,256,1024]{2,1,0:T(8,128)(2,1)} %get-tuple-element.23) | copy-start | bytes 6291460
  103.5 39.1 %copy-start.1 = (bf16[4,256,512]{2,1,0:T(8,128)(2,1)S(1)}, bf16[4,256,512]{2,1,0:T(8,128)(2,1)}, u32[]{:S(2)}) copy-start(bf16[4,256,512]{2,1,0:T(8,128)(2,1)} %get-tuple-element.22) | copy-start | bytes 3145732
  142.6 2.6 %copy-start.3 = (bf16[4,256,1024]{2,1,0:T(8,128)(2,1)S(1)}, bf16[4,256,1024]{2,1,0:T(8,128)(2,1)}, u32[]{:S(2)}) copy-start(bf16[4,256,1024]{2,1,0:T(8,128)(2,1)} %get-tuple-element.19) | copy-start | bytes 6291460
  142.6 2.6 %copy-start.5 = (bf16[4,256,512]{2,1,0:T(8,128)(2,1)S(1)}, bf16[4,256,512]{2,1,0:T(8,128)(2,1)}, u32[]{:S(2)}) copy-start(bf16[4,256,512]{2,1,0:T(8,128)(2,1)} %get-tuple-element.20) | copy-start | bytes 3145732
  145.2 2.6 %copy-start.4 = (bf16[4,256,512]{2,1,0:T(8,128)(2,1)S(1)}, bf16[4,256,512]{2,1,0:T(8,128)(2,1)}, u32[]{:S(2)}) copy-start(bf16[4,256,512]{2,1,0:T(8,128)(2,1)} %get-tuple-element.21) | copy-start | bytes 3145732
  147.8 2.6 %copy-start.2 = (bf16[128,1024]{1,0:T(8,128)(2,1)S(1)}, bf16[128,1024]{1,0:T(8,128)(2,1)}, u32[]{:S(2)}) copy-start(bf16[128,1024]{1,0:T(8,128)(2,1)} %shard_map.122) | copy-start | bytes 786436

commit v5 on v4

--- a/solution.py
+++ b/solution.py
@@ -371,6 +371,18 @@
 def token_pieces(ref):
     rows = ref.shape[1] // HALVES
     return [lambda block, h=h: ref.at[block, pl.ds(h * rows, rows)] for h in range(HALVES)]
+
+
+def upright(row):
+    square = (row.shape[1], row.shape[1])
+    diagonal = lax.broadcasted_iota(jnp.int32, square, 0) == lax.broadcasted_iota(jnp.int32, square, 1)
+    return jnp.sum(jnp.where(diagonal, row, 0.0), 1, keepdims=True)
+
+
+def token_scales(domains, domain_weight):
+    shape = (domain_weight.shape[1], domains.shape[1])
+    picks = lax.broadcasted_iota(jnp.int32, shape, 0) == domains
+    return upright(jnp.sum(jnp.where(picks, upright(domain_weight), 0.0), 0, keepdims=True))
 
 
 def load(sems, *pairs):
@@ -486,7 +498,8 @@
     n,
     capacity,
     targets_ref,
-    scales_ref,
+    domains_ref,
+    domain_weight_ref,
     tables_ref,
     part_in,
     gate_in,
@@ -528,9 +541,12 @@
     spread = Gather(place, token_pieces(grads_ref), send, recv)
     loads[0].wait()
 
+    scales = token_scales(domains_ref[...], domain_weight_ref[...])
+    rows = targets_ref.shape[0] // HALVES
+
     def leave(h, span, total):
         error = total - targets_ref[span, :].astype(f32)
-        grads_ref[place.me, span] = (scales_ref[span, :] * error).astype(bf16)
+        grads_ref[place.me, span] = (scales[h * rows : (h + 1) * rows] * error).astype(bf16)
         spread.begin(h)
 
     begin, steps, finish = scatter(place, part_ref, bufs, sems, leave)
@@ -595,15 +611,20 @@
             copy.wait()
 
 
-def loss_kernel(n, part_ref, targets_ref, scales_ref, grads_ref, *scratch):
+def loss_kernel(
+    n, part_ref, targets_ref, domains_ref, domain_weight_ref, grads_ref, *scratch
+):
     place = Place(n)
     bufs, sems, (send, recv) = scratch[:6], scratch[6:14], scratch[14:]
     greet(place)
     spread = Gather(place, token_pieces(grads_ref), send, recv)
 
+    scales = token_scales(domains_ref[...], domain_weight_ref[...])
+    rows = targets_ref.shape[0] // HALVES
+
     def leave(h, span, total):
         error = total - targets_ref[span, :].astype(jnp.float32)
-        grads_ref[place.me, span] = (scales_ref[span, :] * error).astype(jnp.bfloat16)
+        grads_ref[place.me, span] = (scales[h * rows : (h + 1) * rows] * error).astype(jnp.bfloat16)
         spread.begin(h)
 
     begin, steps, finish = scatter(place, part_ref, bufs, sems, leave)
@@ -711,8 +732,7 @@
         out_vmem=1,
     )
     outs = outs.reshape(n, count, width)
-    picks = domains[:, None] == jnp.arange(domain_weight.shape[0], dtype=jnp.int32)[None, :]
-    scales = jnp.sum(jnp.where(picks, domain_weight[None, :], 0.0), 1, keepdims=True)
+    loss_weights = (domains.reshape(1, -1), domain_weight.reshape(1, -1))
     bufs, sems = scatter_scratch(n, count, width)
     grad_shapes = [
         ((height, slots, width), bf16),
@@ -738,13 +758,13 @@
             + [pltpu.SemaphoreType.DMA((4, height)), pltpu.SemaphoreType.DMA((6,))],
             1,
             targets,
-            scales,
+            *loss_weights,
             tables,
             outs,
             gate_pre,
             up_pre,
             *weights,
-            in_vmem=3,
+            in_vmem=4,
             out_vmem=0,
         )
         slot_grads = slot_grads.reshape(n * capacity, width)
@@ -769,7 +789,7 @@
             1,
             outs,
             targets,
-            scales,
+            *loss_weights,
         )
 
         slot_grads = block_dot(gated, loss_grads, ((2,), (1,))).reshape(n * capacity, width)

time: 151 us -> 150 us (level)
  no operation moved by 1% of the time
where the time goes in v5:
time: 150 us
  Pallas kernels  140 us (93%)
  matrix products  7.79 us (5%)
    pallas_call x3, Pallas kernels, run(): pl.pallas_call(kernel, out_shape=out_shape, in_specs=places(len(operands)...  140 us

profile of v5, /device:TPU:0, one launch (start us, length us, event | category | flops | bytes accessed | tf_op | source)
XLA Modules:
  0.0 149.5 jit_solution(4513848942489099397)
XLA Ops:
  0.6 36.6 %shard_map.120 = (f32[16,32,128]{2,1,0:T(8,128)}, bf16[4,256,1024]{2,1,0:T(8,128)(2,1)}, f32[4,256,512]{2,1,0:T(8,128)}, f32[4,256,512]{2,1,0:T(8,128)}, bf16[4,...) custom-call(bf16[128,1024]{1,0:T(8,128)(2,1)} %tokens_ref.1, s32[6,128]{1,0:T(8,128)} %bitcast.21, ...), custom_call_target="tpu_custom_call" | custom-call | tf_op jit(solution)/shard_map/pallas_call | solution.py:661
  37.3 64.9 %shard_map.121 = (bf16[4,256,1024]{2,1,0:T(8,128)(2,1)}, bf16[4,256,512]{2,1,0:T(8,128)(2,1)}, bf16[4,256,512]{2,1,0:T(8,128)(2,1)}, bf16[16,128,1024]{2,1,0:T(8,128)(2,1)}) custom-call(bf16[128,1024]{1,0:T(8,128)(2,1)} %targets_ref.1, s32[1,128]{1,0:T(1,128)} %bitcast.23, f32[1,64]{1,0:T(1,128)} %bitcast.24, f32[16,32,128]{2,1,0:T(8,128)} %get-tuple-element.14.tables_ref, ...), custom_call_target="tpu_custom_call" | custom-call | tf_op jit(solution)/shard_map/pallas_call | solution.py:661
  102.1 0.0 copy-start
  102.2 0.0 copy-start.1
  102.2 38.8 %shard_map.122 = bf16[128,1024]{1,0:T(8,128)(2,1)} custom-call(bf16[16,128,1024]{2,1,0:T(8,128)(2,1)} %get-tuple-element.18.part_ref), custom_call_target="tpu_custom_call" | custom-call | tf_op jit(solution)/shard_map/pallas_call | solution.py:661
  141.0 0.0 copy-done
  141.0 0.0 copy-done.1
  141.0 0.0 copy-start.3
  141.0 0.0 copy-start.5
  141.0 2.6 %convolution_bitcast_fusion = f32[1,512,1024]{2,1,0:T(8,128)} fusion(bf16[4,256,512]{2,1,0:T(8,128)(2,1)S(1)} %copy-done.1, bf16[4,256,1024]{2,1,0:T(8,128)(2,1)S(1)} %copy-done), kind=kOutput, calls=%fused_computation | convolution fusion | flops 1073741824 | bytes 5242880 | tf_op jit(solution)/shard_map/dot_general | solution.py:810
  143.6 0.0 copy-done.3
  143.6 0.0 copy-done.5
  143.6 0.0 copy-start.4
  143.6 2.6 %convolution_bitcast_fusion.2 = f32[1,1024,512]{2,1,0:T(8,128)} fusion(bf16[4,256,1024]{2,1,0:T(8,128)(2,1)S(1)} %copy-done.3, bf16[4,256,512]{2,1,0:T(8,128)(2,1)S(1)} %copy-done.5), kind=kOutput, calls=%fused_computation.2 | convolution fusion | flops 1073741824 | bytes 5242880 | tf_op jit(solution)/shard_map/dot_general | solution.py:811
  146.2 0.0 copy-done.4
  146.2 0.0 copy-start.2
  146.2 2.6 %convolution_bitcast_fusion.1 = f32[1,1024,512]{2,1,0:T(8,128)} fusion(bf16[4,256,1024]{2,1,0:T(8,128)(2,1)S(1)} %copy-done.3, bf16[4,256,512]{2,1,0:T(8,128)(2,1)S(1)} %copy-done.4), kind=kOutput, calls=%fused_computation.1 | convolution fusion | flops 1073741824 | bytes 5242880 | tf_op jit(solution)/shard_map/dot_general | solution.py:812
  148.8 0.0 copy-done.2
  148.8 0.7 copy.20
Async XLA Ops:
  102.1 38.9 %copy-start = (bf16[4,256,1024]{2,1,0:T(8,128)(2,1)S(1)}, bf16[4,256,1024]{2,1,0:T(8,128)(2,1)}, u32[]{:S(2)}) copy-start(bf16[4,256,1024]{2,1,0:T(8,128)(2,1)} %get-tuple-element.23) | copy-start | bytes 6291460
  102.2 38.9 %copy-start.1 = (bf16[4,256,512]{2,1,0:T(8,128)(2,1)S(1)}, bf16[4,256,512]{2,1,0:T(8,128)(2,1)}, u32[]{:S(2)}) copy-start(bf16[4,256,512]{2,1,0:T(8,128)(2,1)} %get-tuple-element.22) | copy-start | bytes 3145732
  141.0 2.6 %copy-start.3 = (bf16[4,256,1024]{2,1,0:T(8,128)(2,1)S(1)}, bf16[4,256,1024]{2,1,0:T(8,128)(2,1)}, u32[]{:S(2)}) copy-start(bf16[4,256,1024]{2,1,0:T(8,128)(2,1)} %get-tuple-element.19) | copy-start | bytes 6291460
  141.0 2.6 %copy-start.5 = (bf16[4,256,512]{2,1,0:T(8,128)(2,1)S(1)}, bf16[4,256,512]{2,1,0:T(8,128)(2,1)}, u32[]{:S(2)}) copy-start(bf16[4,256,512]{2,1,0:T(8,128)(2,1)} %get-tuple-element.20) | copy-start | bytes 3145732
  143.6 2.6 %copy-start.4 = (bf16[4,256,512]{2,1,0:T(8,128)(2,1)S(1)}, bf16[4,256,512]{2,1,0:T(8,128)(2,1)}, u32[]{:S(2)}) copy-start(bf16[4,256,512]{2,1,0:T(8,128)(2,1)} %get-tuple-element.21) | copy-start | bytes 3145732
  146.2 2.6 %copy-start.2 = (bf16[128,1024]{1,0:T(8,128)(2,1)S(1)}, bf16[128,1024]{1,0:T(8,128)(2,1)}, u32[]{:S(2)}) copy-start(bf16[128,1024]{1,0:T(8,128)(2,1)} %shard_map.122) | copy-start | bytes 786436
